TPU v7x, 512 devices: a whole 4x8x8 slice. The times are simulated.
512 devices in a mesh: dp: 16 (over z_lo, y), section: 8 (over x, core), mp: 4 (over z_hi).
Axes of the slice: x: 4, y: 8, z: 8 (z_hi: 4, z_lo: 2; z = z_hi * 2 + z_lo), core: 2. Of those that a mesh axis runs over, the one named last changes fastest.
Arguments:
- queries: bfloat16 [8, 3072, 4096], P('section', 'dp', 'mp'), may hold values from -30 to 30
- grad_context: bfloat16 [8, 3072, 4096], P('section', 'dp', 'mp'), may hold values from -6 to 6
- encodings: bfloat16 [96, 128, 896], P('dp', ('section', 'mp')), may hold values from -6 to 6
- table: int32 [48, 2], P('dp'), may hold values from 0 to 5
- counts: int32 [48], P('dp'), may hold values from 1 to 2
- key_weight: bfloat16 [8, 896, 4096], P('section', 'dp', 'mp'), may hold values from -0.1875 to 0.1875
- value_weight: bfloat16 [8, 896, 4096], P('section', 'dp', 'mp'), may hold values from -0.1875 to 0.1875
Outputs:
- context: bfloat16 [8, 3072, 4096], P('section', 'dp', 'mp')
- grad_queries: bfloat16 [8, 3072, 4096], P('section', 'dp', 'mp')
- key_grad: float32 [8, 896, 4096], P('section', 'dp', 'mp')
- value_grad: float32 [8, 896, 4096], P('section', 'dp', 'mp')
All inputs are finite; a program needn't handle non-finite values.
Results may differ from a plain program's by a relative error of at most 0.025.
The roundings to bfloat16 on the way count: a program that leaves them out, or rounds other values in their place, can miss the bound.
Values may be sent and summed in bfloat16 or wider, within the bound.
A program may use at most 64 MiB of HBM per device.

v0:
```python
import jax
import jax.numpy as jnp
from jax import lax
from jax.sharding import PartitionSpec as P

HDIM = 128


def grad_rows(flat, slot_grads):
    return jnp.einsum("rk,rm->km", flat, slot_grads, preferred_element_type=jnp.float32)


def body(queries, grad_context, encodings, table, counts, key_weight, value_weight):
    whole = lax.all_gather(encodings, ("section", "mp"), axis=1, tiled=True)
    slots, nlen, width = whole.shape
    flat = whole.reshape(slots * nlen, width)
    local = key_weight.shape[2]
    key_sum = jnp.dot(
        flat,
        lax.all_gather(key_weight[0], "dp", axis=0, tiled=True),
        preferred_element_type=jnp.float32,
    )
    value_sum = jnp.dot(
        flat,
        lax.all_gather(value_weight[0], "dp", axis=0, tiled=True),
        preferred_element_type=jnp.float32,
    )
    keys = key_sum.astype(jnp.bfloat16)
    values = value_sum.astype(jnp.bfloat16)
    heads = local // HDIM
    blocks, neigh = table.shape
    span = queries.shape[1] // blocks
    scale = HDIM ** (-0.5)
    query_heads = queries[0].reshape(blocks, span, heads, HDIM)
    grad_heads = grad_context[0].reshape(blocks, span, heads, HDIM)
    picked_keys = keys.reshape(slots, nlen, heads, HDIM)[table].reshape(
        blocks, neigh * nlen, heads, HDIM
    )
    picked_values = values.reshape(slots, nlen, heads, HDIM)[table].reshape(
        blocks, neigh * nlen, heads, HDIM
    )
    scores = (
        jnp.einsum("cqhd,ckhd->chqk", query_heads, picked_keys, preferred_element_type=jnp.float32)
        * scale
    )
    live = jnp.arange(neigh)[None, :] < counts[:, None]
    live = jnp.repeat(live, nlen, axis=1)
    scores = jnp.where(live[:, None, None, :], scores, jnp.float32(-1e30))
    top = jnp.max(scores, axis=-1, keepdims=True)
    weights = jnp.exp(scores - top)
    probs = weights / jnp.sum(weights, axis=-1, keepdims=True)
    probs_low = probs.astype(jnp.bfloat16)
    context = jnp.einsum(
        "chqk,ckhd->cqhd", probs_low, picked_values, preferred_element_type=jnp.float32
    )
    context = context.reshape(blocks * span, local).astype(jnp.bfloat16)
    onehot = (table[:, :, None] == jnp.arange(slots)[None, None, :]).astype(jnp.float32)
    value_terms = jnp.einsum(
        "chqk,cqhd->ckhd", probs_low, grad_heads, preferred_element_type=jnp.float32
    )
    value_slots = jnp.einsum(
        "cjs,cjnm->snm",
        onehot,
        value_terms.reshape(blocks, neigh, nlen, local),
        precision=lax.Precision.HIGHEST,
    )
    value_slots = value_slots.reshape(slots * nlen, local).astype(jnp.bfloat16)
    dprob = jnp.einsum(
        "cqhd,ckhd->chqk", grad_heads, picked_values, preferred_element_type=jnp.float32
    )
    delta = jnp.sum(probs * dprob, axis=-1, keepdims=True)
    dscore = (probs * (dprob - delta) * scale).astype(jnp.bfloat16)
    grad_queries = jnp.einsum(
        "chqk,ckhd->cqhd", dscore, picked_keys, preferred_element_type=jnp.float32
    )
    grad_queries = grad_queries.reshape(blocks * span, local).astype(jnp.bfloat16)
    key_terms = jnp.einsum(
        "chqk,cqhd->ckhd", dscore, query_heads, preferred_element_type=jnp.float32
    )
    key_slots = jnp.einsum(
        "cjs,cjnm->snm",
        onehot,
        key_terms.reshape(blocks, neigh, nlen, local),
        precision=lax.Precision.HIGHEST,
    )
    key_slots = key_slots.reshape(slots * nlen, local).astype(jnp.bfloat16)
    joined = lax.psum_scatter(
        jnp.concatenate([grad_rows(flat, key_slots), grad_rows(flat, value_slots)], axis=1).astype(
            jnp.bfloat16
        ),
        "dp",
        scatter_dimension=0,
        tiled=True,
    ).astype(jnp.float32)
    key_grad = joined[:, :local]
    value_grad = joined[:, local:]
    return (context[None], grad_queries[None], key_grad[None], value_grad[None])


def solution(mesh):
    in_specs = (
        P("section", "dp", "mp"),
        P("section", "dp", "mp"),
        P("dp", ("section", "mp"), None),
        P("dp", None),
        P("dp"),
        P("section", "dp", "mp"),
        P("section", "dp", "mp"),
    )
    out_specs = (
        P("section", "dp", "mp"),
        P("section", "dp", "mp"),
        P("section", "dp", "mp"),
        P("section", "dp", "mp"),
    )
    return jax.shard_map(body, mesh=mesh, in_specs=in_specs, out_specs=out_specs, check_vma=False)
```

profile of v0, /device:TPU:6, one launch (start us, length us, event | category | flops | bytes accessed | tf_op | source)
XLA Modules:
  0.0 390.7 jit_solution(12623564279535972196)
XLA Ops:
  7.2 1.4 copy.58
  11.8 1.8 copy.87
  13.6 1.1 copy.89
  14.8 60.1 %all-gather.6.cloned.1.call-done = bf16[6,128,896]{2,0,1:T(8,128)(2,1)} async-done(((bf16[6,4,896]{2,0,1:T(8,128)(2,1)}), bf16[6,128,896]{2,0,1:T(8,128)(2,1)}) %all-gather.6.cloned.1.call-update) | async-done | bytes 1376272 | tf_op jit(solution)/shard_map/all_gather | solution.py:14
  74.9 1.7 copy.59
  76.6 72.7 %all-gather.8.cloned.1.call-done = bf16[1,896,1024]{2,1,0:T(8,128)(2,1)} async-done(((bf16[1,56,1024]{2,1,0:T(8,128)(2,1)}), bf16[1,896,1024]{2,1,0:T(8,128)(2,1)}) %all-gather.8.cloned.1.call-update) | async-done | bytes 1835024 | tf_op jit(solution)/shard_map/all_gather | solution.py:25
  149.4 3.3 fusion.39
  153.1 69.6 %all-gather.10.cloned.1.call-done = bf16[1,896,1024]{2,1,0:T(8,128)(2,1)} async-done(((bf16[1,56,1024]{2,1,0:T(8,128)(2,1)}), bf16[1,896,1024]{2,1,0:T(8,128)(2,1)}) %all-gather.10.cloned.1.call-update) | async-done | bytes 1835024 | tf_op jit(solution)/shard_map/all_gather | solution.py:20
  222.8 3.3 fusion.36
  226.1 1.6 copy.86
  228.5 2.8 gather_fusion.1
  231.4 1.9 multiply_select_fusion
  233.3 1.7 fusion.86
  235.7 6.9 %convolution_bitcast_fusion = f32[3,256,8,128]{3,1,2,0:T(8,128)} fusion(bf16[3,64,8,128]{3,2,1,0:T(8,128)(2,1)S(1)} %bitcast.123, f32[3,8,64]{2,1,0:T(8,128)S(1)} %get-tuple-element.22, f32[3,8,256,64]{2,3,1,0:T(8,128)} %copy-done.5), kind=kOutput, calls=%fused_computation.13 | convolution fusion | flops 101844736 | bytes 5117952 | tf_op jit(solution)/shard_map/chqk,cqhd->ckhd/dot_general | solution.py:58
  242.6 12.8 %convolution_bitcast_fusion.1 = f32[3,256,8,128]{3,1,2,0:T(8,128)} fusion(f32[3,8,256,64]{2,3,1,0:T(8,128)S(1)} %fusion.42, bf16[3,64,8,128]{3,2,1,0:T(8,128)(2,1)S(1)} %bitcast.131, f32[3,8,64,256]{3,2,1,0:T(8,128)} %get-tuple-element.23, f32[3,8,64]{2,1,0:T(8,128)S(1)} %get-tuple-element.22), kind=kOutput, calls=%fused_computation.14 | convolution fusion | flops 103417600 | bytes 6690816 | tf_op jit(solution)/shard_map/chqk,cqhd->ckhd/dot_general | solution.py:77
  255.4 3.7 copy.71
  259.2 2.5 reshape.68
  261.7 10.3 %bitcast_convert_fusion.1 = bf16[6,128,1024]{2,0,1:T(8,128)(2,1)S(1)} fusion(f32[3,2,128,1024]{3,2,1,0:T(8,128)} %reshape.68, s32[3,2]{1,0:T(4,128)S(1)} %copy.69), kind=kOutput, calls=%fused_computation.5 | convolution fusion | flops 57409572 | bytes 4718616 | tf_op jit(solution)/shard_map/cjs,cjnm->snm/dot_general | solution.py:80
  272.0 3.9 fusion.27
  275.9 1.8 copy.76
  277.7 2.3 reshape.69
  280.0 10.3 %bitcast_convert_fusion = bf16[6,128,1024]{2,0,1:T(8,128)(2,1)S(1)} fusion(f32[3,2,128,1024]{3,2,1,0:T(8,128)} %reshape.69, s32[3,2]{1,0:T(4,128)S(1)} %copy.69), kind=kOutput, calls=%fused_computation.4 | convolution fusion | flops 57409572 | bytes 4718616 | tf_op jit(solution)/shard_map/cjs,cjnm->snm/dot_general | solution.py:61
  290.4 2.6 fusion.30
  293.0 2.1 pad_maximum_fusion
  295.1 6.2 %copy.84 = bf16[896,2048]{1,0:T(8,128)(2,1)} copy(bf16[896,2048]{0,1:T(8,128)(2,1)} %pad_maximum_fusion) | data formatting | bytes 7340032
  301.3 1.4 copy-done.7
  302.7 11.3 %fusion.58 = bf16[3,64,8,128]{3,1,2,0:T(8,128)(2,1)S(1)} fusion(bf16[3,256,8,128]{3,2,1,0:T(8,128)(2,1)S(1)} %bitcast.125, f32[3,8,256,64]{2,3,1,0:T(8,128)} %copy-done.4, f32[3,8,64,256]{3,2,1,0:T(8,128)} %get-tuple-element.23, f32[3,8,64]{2,1,0:T(8,128)S(1)} %get-tuple-element.22), kind=kOutput, calls=%fused_computation.47 | convolution fusion | flops 103614208 | bytes 5117952 | tf_op jit(solution)/shard_map/chqk,ckhd->cqhd/dot_general | solution.py:73
  314.3 0.9 convert_element_type.66
  315.2 4.2 %fusion.55 = bf16[3,64,8,128]{3,1,2,0:T(8,128)(2,1)S(1)} fusion(bf16[3,256,8,128]{3,2,1,0:T(8,128)(2,1)S(1)} %bitcast.119, f32[3,8,64]{2,1,0:T(8,128)S(1)} %get-tuple-element.22, f32[3,8,256,64]{2,3,1,0:T(8,128)} %copy-done.5), kind=kOutput, calls=%fused_computation.46 | convolution fusion | flops 102041344 | bytes 3545088 | tf_op jit(solution)/shard_map/chqk,ckhd->cqhd/dot_general | solution.py:53
  319.7 0.9 convert_element_type.62
  320.6 60.5 %reduce-scatter.4.cloned.1.call-done = bf16[56,2048]{1,0:T(8,128)(2,1)} async-done(((bf16[896,2048]{1,0:T(8,128)(2,1)}), bf16[56,2048]{1,0:T(8,128)(2,1)}) %reduce-scatter.4.cloned.1.call-update) | async-done | bytes 229392
  381.0 1.2 copy.85
  (49 shorter events, 7.7 us)
Async XLA Ops:
  7.2 7.6 %copy-start.12 = (s32[3]{0:T(128)S(1)}, s32[3]{0:T(128)}, u32[]{:S(2)}) copy-start(s32[3]{0:T(128)} %param.11) | copy-start | bytes 40
  7.2 67.8 %all-gather.6.cloned.1.call-start = ((), (), s32[]{:S(2)}) async-start(), calls=%async_computation.1 | async-start | bytes 1892352 | tf_op jit(solution)/shard_map/all_gather | solution.py:14
  8.7 140.7 %all-gather.8.cloned.1.call-start = ((), (), s32[]{:S(2)}) async-start(), calls=%async_computation.2 | async-start | bytes 1949696 | tf_op jit(solution)/shard_map/all_gather | solution.py:25
  9.4 213.3 %all-gather.10.cloned.1.call-start = ((), (), s32[]{:S(2)}) async-start(), calls=%async_computation.3 | async-start | bytes 1949696 | tf_op jit(solution)/shard_map/all_gather | solution.py:20
  10.1 370.9 %reduce-scatter.4.cloned.1.call-start = ((), (), s32[]{:S(2)}) async-start(), calls=%async_computation.4 | async-start | bytes 3899392
  76.6 146.1 %copy-start.8 = (bf16[6,128,896]{2,1,0:T(8,128)(2,1)}, bf16[6,128,896]{2,1,0:T(8,128)(2,1)S(1)}, u32[]{:S(2)}) copy-start(bf16[6,128,896]{2,1,0:T(8,128)(2,1)S(1)} %copy.59) | copy-start | bytes 4128772
  228.5 6.5 %copy-start = (bf16[6,128,8,128]{3,2,1,0:T(8,128)(2,1)}, bf16[6,128,8,128]{3,2,1,0:T(8,128)(2,1)S(1)}, u32[]{:S(2)}) copy-start(bf16[6,128,8,128]{3,2,1,0:T(8,128)(2,1)S(1)} %gather_fusion) | copy-start | bytes 4718596
  231.4 2.0 copy-start.6
  233.3 1.7 copy-start.5
  235.7 6.9 %copy-start.4 = (f32[3,8,256,64]{2,3,1,0:T(8,128)}, f32[3,8,256,64]{2,3,1,0:T(8,128)S(1)}, u32[]{:S(2)}) copy-start(f32[3,8,256,64]{2,3,1,0:T(8,128)S(1)} %fusion.42) | copy-start | bytes 4718596
  235.7 6.9 %copy-start.11 = (bf16[24,8,8,128]{3,2,1,0:T(8,128)(2,1)S(1)}, bf16[24,8,8,128]{3,2,1,0:T(8,128)(2,1)}, u32[]{:S(2)}) copy-start(bf16[24,8,8,128]{3,2,1,0:T(8,128)(2,1)} %copy.87) | copy-start | bytes 1179652
  261.7 10.3 %copy-start.9 = (bf16[6,128,896]{2,1,0:T(8,128)(2,1)S(1)}, bf16[6,128,896]{2,1,0:T(8,128)(2,1)}, u32[]{:S(2)}) copy-start(bf16[6,128,896]{2,1,0:T(8,128)(2,1)} %copy-done.8) | copy-start | bytes 4128772
  272.0 3.9 copy-start.2
  280.0 10.3 %copy-start.10 = (bf16[6,128,896]{2,1,0:T(8,128)(2,1)S(1)}, bf16[6,128,896]{2,1,0:T(8,128)(2,1)}, u32[]{:S(2)}) copy-start(bf16[6,128,896]{2,1,0:T(8,128)(2,1)} %copy-done.8) | copy-start | bytes 4128772
  290.3 2.6 copy-start.3
  301.3 1.4 copy-start.7
  302.7 12.5 %copy-start.1 = (bf16[6,128,8,128]{3,2,1,0:T(8,128)(2,1)S(1)}, bf16[6,128,8,128]{3,2,1,0:T(8,128)(2,1)}, u32[]{:S(2)}) copy-start(bf16[6,128,8,128]{3,2,1,0:T(8,128)(2,1)} %copy-done) | copy-start | bytes 4718596
Sparse Core Ops, SparseCore 0:
  11.8 63.1 all-gather.5
  77.0 72.3 all-gather.7
  151.5 71.2 all-gather.9
  301.4 79.5 reduce-scatter.3
where the time goes:
time: 391 us
  waiting for transfers between devices  264 us (68%)
  matrix products  71.5 us (18%)
  local copies, waits for them, and re-layouts  36 us (9%)
  between operations  14 us (4%)
  other arithmetic  4.59 us (1%)
    all_gather x1, waiting for transfers between devices, body(): lax.all_gather(value_weight[0], 'dp', axis=0, tiled=True)  72.7 us
    all_gather x1, waiting for transfers between devices, body(): lax.all_gather(key_weight[0], 'dp', axis=0, tiled=True)  69.6 us
    unnamed x5, waiting for transfers between devices  61.9 us
    all_gather x1, waiting for transfers between devices, body(): whole = lax.all_gather(encodings, ('section', 'mp'), axis=1, tiled=True)  60.1 us
    unnamed x36, local copies, waits for them, and re-layouts  17.7 us
    dot_general x1, matrix products, body(): jnp.einsum('chqk,cqhd->ckhd', dscore, query_heads, preferred_element_type...  12.8 us
    dot_general x1, matrix products, body(): jnp.einsum('chqk,ckhd->cqhd', dscore, picked_keys, preferred_element_type...  11.3 us
    dot_general x1, matrix products, body(): jnp.einsum('cjs,cjnm->snm', onehot, key_terms.reshape(blocks, neigh, nlen...  10.3 us
  transfers between devices with their start and end apart: 4, of which 4 were waited for; matrix products, arithmetic and copies ran while one was open for 7% of the time, Pallas kernels for 0%

commit v1 on v0

v1 whole, which is shorter than its diff:
```python
import functools

import jax
import jax.numpy as jnp
import numpy as np
from jax import lax
from jax.experimental import pallas as pl
from jax.experimental.pallas import tpu as pltpu
from jax.sharding import PartitionSpec as P

MESH = pl.DeviceIdType.MESH
F32, BF16 = jnp.float32, jnp.bfloat16
HDIM = 128
LOG2E = 1.4426950408889634
NY, NX, NZH, NZ = 8, 4, 4, 8
HEADS = 4
SLOTS, PIECE, ENC = 6, 4, 896
CHUNK = SLOTS * PIECE
TOKENS = 768
ROWS, BLOCK, BLOCKS = 192, 64, 3
WROWS = 56
ZORDER = (0, 1, 7, 2, 6, 3, 5, 4)


def mod(value, n):
    return lax.rem(value + n, n)


def kernel(
    table_ref, counts_ref, slot_ref, q_ref, g_ref, enc_ref, wk_ref, wv_ref,
    ctx_out, gq_out, kg_out, vg_out,
    ebuf, tok, tok_t, wraw, qg, mult, keys, values, probs_s, dscore_s, slots_s, terms, landed, stage, total,
    mult_sem, z_send, z_recv, xp_send, xp_recv, xm_send, xm_recv, xo_send, xo_recv, sib_send, sib_recv,
    wl_sem, wz_send, wz_recv, wy_send, wy_recv, ql_sem, qz_send, qz_recv, rs_send, rs_recv,
    ol_sem, oz_send, oz_recv, fl_sem, fz_send, fz_recv,
):
    dp, section, zh = lax.axis_index("dp"), lax.axis_index("section"), lax.axis_index("mp")
    zl, y = dp // NY, lax.rem(dp, NY)
    x, core = section // 2, lax.rem(section, 2)
    z = zh * 2 + zl
    other = 1 - zl

    partner = {"dp": other * NY + y}
    sibling = {"section": x * 2 + 1 - core}

    def at_y(step):
        return {"dp": zl * NY + mod(y + step, NY)}

    def at_x(step):
        return {"section": mod(x + step, NX) * 2 + core}

    def at_z(step):
        there = mod(z + step, NZ)
        return {"dp": lax.rem(there, 2) * NY + y, "mp": there // 2}

    def remote(src, dst, send, recv, device):
        return pltpu.make_async_remote_copy(
            src_ref=src, dst_ref=dst, send_sem=send, recv_sem=recv, device_id=device, device_id_type=MESH
        )

    sent = []

    def push(src, dst, send, recv, device):
        copy = remote(src, dst, send, recv, device)
        copy.start()
        sent.append(copy)

    def arrived(ref, recv):
        remote(ref, ref, recv, recv, sibling).wait_recv()

    barrier = pltpu.get_barrier_semaphore()
    friends = [at_z(d) for d in range(1, NZ)] + [at_x(1), at_x(-1), sibling, at_y(1), at_y(-1)]
    for friend in friends:
        pl.semaphore_signal(barrier, inc=1, device_id=friend, device_id_type=MESH)

    def own_columns(h):
        return pl.ds(pl.multiple_of(zl * HEADS * HDIM + h * HDIM, HDIM), HDIM)

    def other_columns(h):
        return pl.ds(pl.multiple_of(other * HEADS * HDIM + h * HDIM, HDIM), HDIM)

    local = []
    for h in range(HEADS):
        for i, w_ref in enumerate((wk_ref, wv_ref)):
            copy = pltpu.make_async_copy(
                w_ref.at[0, :, own_columns(h)], wraw.at[h, zl, y, :, pl.ds(i * HDIM, HDIM)], wl_sem.at[h, i]
            )
            copy.start()
            local.append(copy)
    local_q = []
    for h in range(HEADS):
        for i, w_ref in enumerate((q_ref, g_ref)):
            copy = pltpu.make_async_copy(w_ref.at[0, :, own_columns(h)], qg.at[0, h, i], ql_sem.at[h, i])
            copy.start()
            local_q.append(copy)
    pieces = [enc_ref[s].astype(F32) for s in range(SLOTS)]
    ebuf[zl, zh, x, core] = jnp.concatenate(pieces, axis=0).astype(BF16)
    slot_of = slot_ref[...]
    for c in range(BLOCKS):
        times = jnp.where(slot_of == table_ref[c, 0], 1.0, 0.0)
        second = jnp.where(counts_ref[c] > 1, 1.0, 0.0)
        mult[0, c] = times + jnp.where(slot_of == table_ref[c, 1], 1.0, 0.0) * second

    pl.semaphore_wait(barrier, len(friends))

    def chunk(dz, dx, core_of):
        zz = mod(z + dz, NZ)
        return ebuf.at[lax.rem(zz, 2), zz // 2, mod(x + dx, NX), core_of]

    mine = chunk(0, 0, core)
    for d in ZORDER[1:]:
        push(mine, mine, z_send.at[d], z_recv.at[d], at_z(d))
    for h in range(HEADS):
        for i, w_ref in enumerate((wk_ref, wv_ref)):
            push(
                w_ref.at[0, :, other_columns(h)], wraw.at[h, zl, y, :, pl.ds(i * HDIM, HDIM)],
                wz_send.at[h, i], wz_recv.at[h, i], partner,
            )
    push(mult.at[0], mult.at[1], mult_sem.at[0], mult_sem.at[1], partner)
    for h in range(HEADS):
        for i, w_ref in enumerate((q_ref, g_ref)):
            push(w_ref.at[0, :, other_columns(h)], qg.at[1, h, i], qz_send.at[h, i], qz_recv.at[h, i], partner)

    def w_step(h, t):
        way = 1 if h % 2 == 0 else -1
        if t == 0:
            for i in range(2):
                local[h * 2 + i].wait()
                arrived(wraw.at[h, other, y, :, pl.ds(i * HDIM, HDIM)], wz_recv.at[h, i])
        else:
            arrived(wraw.at[h, :, mod(y - way * t, NY)], wy_recv.at[h, t - 1])
        if t < 4:
            there = wraw.at[h, :, mod(y - way * t, NY)]
            push(there, there, wy_send.at[h, t], wy_recv.at[h, t], at_y(way))
        if 0 < t < 4:
            arrived(wraw.at[h, :, mod(y + way * t, NY)], wy_recv.at[h, 3 + t])
        if t < 3:
            there = wraw.at[h, :, mod(y + way * t, NY)]
            push(there, there, wy_send.at[h, 4 + t], wy_recv.at[h, 4 + t], at_y(-way))

    def to_sibling(ref, d, dx):
        i = d * NX + dx
        push(ref, ref, sib_send.at[i], sib_recv.at[i], sibling)

    def e_first(d):
        ref = chunk(-d, 0, core)
        if d:
            arrived(ref, z_recv.at[d])
        push(ref, ref, xp_send.at[d], xp_recv.at[d], at_x(1))
        push(ref, ref, xm_send.at[d], xm_recv.at[d], at_x(-1))
        to_sibling(ref, d, 0)

    def e_second(d):
        ref = chunk(-d, -1, core)
        arrived(ref, xp_recv.at[d])
        if d % 2 == 0:
            push(ref, ref, xo_send.at[d], xo_recv.at[d], at_x(1))
        to_sibling(ref, d, 3)
        ref = chunk(-d, 1, core)
        arrived(ref, xm_recv.at[d])
        if d % 2 == 1:
            push(ref, ref, xo_send.at[d], xo_recv.at[d], at_x(-1))
        to_sibling(ref, d, 1)

    def e_third(d):
        ref = chunk(-d, 2, core)
        arrived(ref, xo_recv.at[d])
        to_sibling(ref, d, 2)

    turns = [(0,), (1, 7), (2, 6), (3, 5), (4,)]
    w_turns = [
        [(0, 0), (1, 0)], [(0, 1), (1, 1)], [(0, 2), (1, 2)], [(0, 3), (1, 3), (2, 0)], [(0, 4), (1, 4), (3, 0)],
        [(2, 1), (3, 1)], [(2, 2), (3, 2)], [(2, 3), (3, 3)], [(2, 4), (3, 4)],
    ]
    for turn in range(9):
        for stage_of, behind in ((e_first, 0), (e_second, 2), (e_third, 4)):
            if 0 <= turn - behind < len(turns):
                for d in turns[turn - behind]:
                    stage_of(d)
        for h, t in w_turns[turn]:
            w_step(h, t)
    for d in range(NZ):
        for dx in range(NX):
            arrived(chunk(-d, dx, 1 - core), sib_recv.at[d * NX + dx])
    for copy in local_q:
        copy.wait()
    for h in range(HEADS):
        for i in range(2):
            arrived(qg.at[1, h, i], qz_recv.at[h, i])
    arrived(mult.at[1], mult_sem.at[1])

    for r in range(2):

        @pl.loop(0, NZH)
        def _(zz):
            part = ebuf[r, zz].reshape(NX * 2, CHUNK, ENC).astype(F32).reshape(NX * 2 * CHUNK, ENC)
            span = pl.ds(pl.multiple_of(zz * NX * 2 * CHUNK, NX * 2 * CHUNK), NX * 2 * CHUNK)
            tok[r, span, :] = part.astype(BF16)

        @pl.loop(0, 7)
        def _(i):
            span = pl.ds(pl.multiple_of(i * HDIM, HDIM), HDIM)
            tok_t[r, span, :] = tok[r, :, span].T

    scale = HDIM**-0.5

    def project(h):
        w = wraw[h].reshape(2 * NY * WROWS, 2 * HDIM)
        for r in range(2):

            @pl.loop(0, 3)
            def _(i):
                span = pl.ds(pl.multiple_of(i * 256, 256), 256)
                kv = jnp.dot(tok[r, span, :], w, preferred_element_type=F32).astype(BF16)
                keys[r, span, :] = kv[:, :HDIM]
                values[r, span, :] = kv[:, HDIM:]

    def nt(a, b):
        return lax.dot_general(a, b, (((1,), (1,)), ((), ())), preferred_element_type=F32)

    def tn(a, b):
        return lax.dot_general(a, b, (((0,), (0,)), ((), ())), preferred_element_type=F32)

    def attend(h, near):
        r = zl if near == 0 else other

        @pl.loop(0, BLOCKS)
        def _(c):
            k, v = keys[r], values[r]
            span = pl.ds(pl.multiple_of(c * BLOCK, BLOCK), BLOCK)
            q, g = qg[near, h, 0, span, :], qg[near, h, 1, span, :]
            m = mult[near, c, pl.ds(0, 1), :]
            scores = nt(q, k) + jnp.where(m > 0.0, 0.0, -1e30)
            top = jnp.max(scores, axis=1, keepdims=True)
            weights = jnp.exp2((scores - top) * (scale * LOG2E)) * m
            probs = weights / jnp.sum(weights, axis=1, keepdims=True)
            probs_s[span, :] = probs.astype(BF16)
            dprob = nt(g, v)
            delta = jnp.sum(probs * dprob, axis=1, keepdims=True)
            dscore_s[span, :] = (probs * (dprob - delta) * scale).astype(BF16)

        k, v = keys[r], values[r]
        p, s = probs_s[...], dscore_s[...]
        q, g = qg[near, h, 0], qg[near, h, 1]
        stage[near, h, 0] = jnp.dot(p, v, preferred_element_type=F32).astype(BF16)
        stage[near, h, 1] = jnp.dot(s, k, preferred_element_type=F32).astype(BF16)
        slots_s[r, :, pl.ds(0, HDIM)] = tn(s, q).astype(BF16)
        slots_s[r, :, pl.ds(HDIM, HDIM)] = tn(p, g).astype(BF16)
        for i, out in enumerate((ctx_out, gq_out)):
            there = out.at[0, :, own_columns(h)]
            if near:
                push(stage.at[1, h, i], there, oz_send.at[h, i], oz_recv.at[h, i], partner)
            else:
                copy = pltpu.make_async_copy(stage.at[0, h, i], there, ol_sem.at[h, i])
                copy.start()
                ends.append(copy)

    ends = []

    def term(h):
        for half in range(2):
            span = pl.ds(half * NY * WROWS, NY * WROWS)
            both = jnp.dot(tok_t[0, span, :], slots_s[0], preferred_element_type=F32)
            both += jnp.dot(tok_t[1, span, :], slots_s[1], preferred_element_type=F32)
            terms[h, half] = both.reshape(NY, WROWS, 2 * HDIM).astype(BF16)

    def rs_step(h, t):
        way = 1 if h % 2 == 0 else -1
        if t < 4:
            there = mod(y + way * (4 - t), NY)
            if t > 0:
                arrived(landed.at[h, t - 1], rs_recv.at[h, t - 1])
                terms[h, :, there] = (terms[h, :, there].astype(F32) + landed[h, t - 1].astype(F32)).astype(BF16)
            push(terms.at[h, :, there], landed.at[h, t], rs_send.at[h, t], rs_recv.at[h, t], at_y(way))
        if t < 3:
            there = mod(y - way * (3 - t), NY)
            if t > 0:
                arrived(landed.at[h, 3 + t], rs_recv.at[h, 3 + t])
                terms[h, :, there] = (terms[h, :, there].astype(F32) + landed[h, 3 + t].astype(F32)).astype(BF16)
            push(terms.at[h, :, there], landed.at[h, 4 + t], rs_send.at[h, 4 + t], rs_recv.at[h, 4 + t], at_y(-way))
        if t == 4:
            arrived(landed.at[h, 3], rs_recv.at[h, 3])
            arrived(landed.at[h, 6], rs_recv.at[h, 6])
            total[h] = terms[h, :, y].astype(F32) + landed[h, 3].astype(F32) + landed[h, 6].astype(F32)
            for i, out in enumerate((kg_out, vg_out)):
                there = out.at[0, :, own_columns(h)]
                half = pl.ds(i * HDIM, HDIM)
                push(total.at[h, other, :, half], there, fz_send.at[h, i], fz_recv.at[h, i], partner)
                copy = pltpu.make_async_copy(total.at[h, zl, :, half], there, fl_sem.at[h, i])
                copy.start()
                ends.append(copy)

    for h in range(HEADS):
        project(h)
        if h:
            rs_step(h - 1, 1)
        attend(h, 1)
        if h:
            rs_step(h - 1, 2)
        attend(h, 0)
        if h:
            rs_step(h - 1, 3)
        term(h)
        if h:
            rs_step(h - 1, 4)
        rs_step(h, 0)
    for t in range(1, 5):
        rs_step(HEADS - 1, t)

    for h in range(HEADS):
        for i, (out, grad) in enumerate(((ctx_out, kg_out), (gq_out, vg_out))):
            arrived(out.at[0, :, other_columns(h)], oz_recv.at[h, i])
            arrived(grad.at[0, :, other_columns(h)], fz_recv.at[h, i])
    for copy in ends:
        copy.wait()
    for copy in sent:
        copy.wait_send()


def body(queries, grad_context, encodings, table, counts, key_weight, value_weight):
    slot_of = np.broadcast_to((np.arange(TOKENS) % CHUNK // PIECE).astype(np.int32), (8, TOKENS))
    any_ref = pl.BlockSpec(memory_space=pl.ANY)
    vmem = pl.BlockSpec(memory_space=pltpu.VMEM)
    smem = pl.BlockSpec(memory_space=pltpu.SMEM)
    dma = pltpu.SemaphoreType.DMA
    ring = dma((HEADS, 7))
    pair = dma((HEADS, 2))
    eight = dma((NZ,))
    local = key_weight.shape[2]
    scratch = [
        pltpu.VMEM((2, NZH, NX, 2, CHUNK, ENC), BF16),
        pltpu.VMEM((2, TOKENS, ENC), BF16),
        pltpu.VMEM((2, ENC, TOKENS), BF16),
        pltpu.VMEM((HEADS, 2, NY, WROWS, 2 * HDIM), BF16),
        pltpu.VMEM((2, HEADS, 2, ROWS, HDIM), BF16),
        pltpu.VMEM((2, BLOCKS, 8, TOKENS), F32),
        pltpu.VMEM((2, TOKENS, HDIM), BF16),
        pltpu.VMEM((2, TOKENS, HDIM), BF16),
        pltpu.VMEM((ROWS, TOKENS), BF16),
        pltpu.VMEM((ROWS, TOKENS), BF16),
        pltpu.VMEM((2, TOKENS, 2 * HDIM), BF16),
        pltpu.VMEM((HEADS, 2, NY, WROWS, 2 * HDIM), BF16),
        pltpu.VMEM((HEADS, 7, 2, WROWS, 2 * HDIM), BF16),
        pltpu.VMEM((2, HEADS, 2, ROWS, HDIM), BF16),
        pltpu.VMEM((HEADS, 2, WROWS, 2 * HDIM), F32),
        dma((2,)), eight, eight, eight, eight, eight, eight, eight, eight, dma((NZ * NX,)), dma((NZ * NX,)),
        pair, pair, pair, ring, ring, pair, pair, pair, ring, ring,
        pair, pair, pair, pair, pair, pair,
    ]
    return pl.pallas_call(
        kernel,
        out_shape=(
            jax.ShapeDtypeStruct((1, ROWS, local), BF16),
            jax.ShapeDtypeStruct((1, ROWS, local), BF16),
            jax.ShapeDtypeStruct((1, WROWS, local), F32),
            jax.ShapeDtypeStruct((1, WROWS, local), F32),
        ),
        in_specs=[smem, smem, vmem, any_ref, any_ref, vmem, any_ref, any_ref],
        out_specs=(any_ref,) * 4,
        scratch_shapes=scratch,
        compiler_params=pltpu.CompilerParams(
            collective_id=0, has_side_effects=True, vmem_limit_bytes=56 * 1024 * 1024
        ),
    )(table, counts, slot_of, queries, grad_context, encodings, key_weight, value_weight)


def solution(mesh):
    in_specs = (
        P("section", "dp", "mp"),
        P("section", "dp", "mp"),
        P("dp", ("section", "mp"), None),
        P("dp", None),
        P("dp"),
        P("section", "dp", "mp"),
        P("section", "dp", "mp"),
    )
    out_specs = (
        P("section", "dp", "mp"),
        P("section", "dp", "mp"),
        P("section", "dp", "mp"),
        P("section", "dp", "mp"),
    )
    return jax.shard_map(body, mesh=mesh, in_specs=in_specs, out_specs=out_specs, check_vma=False)
```

time: 391 us -> 131 us (0.34)
  waiting for transfers between devices: 264 us -> 0 us
  Pallas kernels: 0 us -> 123 us
  matrix products: 71.5 us -> 0 us
  local copies, waits for them, and re-layouts: 36 us -> 7.24 us
  between operations: 14 us -> 0.65 us
  other arithmetic: 4.59 us -> 0 us
    all_gather x3 -> x0, waiting for transfers between devices: 202 us -> none  [the longest x1 72.7 us: body(): lax.all_gather(value_weight[0], 'dp', axis=0, tiled=True)]
    pallas_call x0 -> x1, Pallas kernels: none -> 123 us  [body(): pl.pallas_call(kernel, out_shape=(jax.ShapeDtypeStruct((1, ROWS, local),...]
    dot_general x12 -> x0, matrix products: 71.5 us -> none  [the longest x1 12.8 us: body(): jnp.einsum('chqk,cqhd->ckhd', dscore, query_heads, preferred_element_type...]
    unnamed x5 -> x0, waiting for transfers between devices: 61.9 us -> none
    unnamed x36 -> x11, local copies, waits for them, and re-layouts: 17.7 us -> 5.95 us
    transpose x2 -> x0, local copies, waits for them, and re-layouts: 5.54 us -> none  [the longest x1 3.71 us: body(): jnp.einsum('chqk,cqhd->ckhd', dscore, query_heads, preferred_element_type...]
    reshape x2 -> x0, local copies, waits for them, and re-layouts: 4.81 us -> none  [the longest x1 2.51 us: body(): key_terms.reshape(blocks, neigh, nlen, local)]
  transfers between devices with their start and end apart: 4 -> 0, of which waited for: 4 -> 0; matrix products, arithmetic and copies ran while one was open for 7% -> 0% of each run, Pallas kernels for 0% -> 0%
where the time goes in v1:
time: 131 us
  Pallas kernels  123 us (94%)
  local copies, waits for them, and re-layouts  7.24 us (6%)
    pallas_call x1, Pallas kernels, body(): pl.pallas_call(kernel, out_shape=(jax.ShapeDtypeStruct((1, ROWS, local),...  123 us
    unnamed x11, local copies, waits for them, and re-layouts  5.95 us

profile of v1, /device:TPU:6, one launch (start us, length us, event | category | flops | bytes accessed | tf_op | source)
XLA Modules:
  0.0 130.7 jit_solution(2211928116329837035)
XLA Ops:
  0.6 1.3 %copy.12.table_ref = s32[3,2]{1,0:T(4,128)} copy(s32[3,2]{0,1:T(2,128)} %param.11) | data formatting | bytes 48 | tf_op args[3]
  2.0 1.3 jit_solution_.3.slot_ref
  3.3 122.8 %shard_map.111 = (bf16[1,192,1024]{2,1,0:T(8,128)(2,1)}, bf16[1,192,1024]{2,1,0:T(8,128)(2,1)}, f32[1,56,1024]{2,1,0:T(8,128)}, f32[1,56,1024]{2,1,0:T(8,128)}) custom-call(s32[3,2]{1,0:T(4,128)} %copy.12.table_ref, s32[3]{0:T(128)} %counts_ref.1, s32[8,768]{1,0:T(8,128)} %jit_solution_.3.slot_ref, bf16[1,192,1024]{2,1,0:T(8,128)(2,1)} %q_ref.1, ...), custom_call_target="tpu_custom_call" | custom-call | tf_op jit(solution)/shard_map/pallas_call | solution.py:350
  126.0 0.0 copy-start
  126.1 1.8 %copy.17 = bf16[1,192,1024]{2,1,0:T(8,128)(2,1)} copy(bf16[1,192,1024]{2,1,0:T(8,128)(2,1)} %get-tuple-element.8) | data formatting | bytes 786432
  127.9 0.0 copy-done
  127.9 0.0 copy-start.2
  127.9 0.7 copy.18
  128.6 0.3 copy-done.2
  129.0 0.0 copy-start.1
  129.0 0.7 copy.19
  129.7 0.3 copy-done.1
  130.0 0.7 copy.20
Async XLA Ops:
  126.0 1.8 %copy-start = (bf16[1,192,1024]{2,1,0:T(8,128)(2,1)S(1)}, bf16[1,192,1024]{2,1,0:T(8,128)(2,1)}, u32[]{:S(2)}) copy-start(bf16[1,192,1024]{2,1,0:T(8,128)(2,1)} %get-tuple-element.9) | copy-start | bytes 1179652
  127.9 1.1 copy-start.2
  129.0 1.0 copy-start.1

commit v2 on v1

v2 whole, which is shorter than its diff:
```python
import functools

import jax
import jax.numpy as jnp
from jax import lax
from jax.experimental import pallas as pl
from jax.experimental.pallas import tpu as pltpu
from jax.sharding import PartitionSpec as P

MESH = pl.DeviceIdType.MESH
F32, BF16 = jnp.float32, jnp.bfloat16
HDIM = 128
LOG2E = 1.4426950408889634
NY, NX, NZH, NZ = 8, 4, 4, 8
HEADS = 4
SLOTS, PIECE, ENC = 6, 4, 896
CHUNK = SLOTS * PIECE
TOKENS = 768
ROWS, BLOCK, BLOCKS = 192, 64, 3
WROWS = 56


def mod(value, n):
    return lax.rem(value + n, n)


def kernel(
    table_ref, counts_ref, q_ref, g_ref, enc_ref, wk_ref, wv_ref,
    ctx_out, gq_out, kg_out, vg_out,
    ebuf, tok, wraw, qg, mult, times, keys, values, slots_t, terms, landed, stage, total,
    mult_sem, z_send, z_recv, xp_send, xp_recv, xm_send, xm_recv, xo_send, xo_recv, sib_send, sib_recv,
    wl_sem, wz_send, wz_recv, wy_send, wy_recv, ql_sem, qz_send, qz_recv, rs_send, rs_recv,
    ol_sem, oz_send, oz_recv, fl_sem, fz_send, fz_recv,
):
    dp, section, zh = lax.axis_index("dp"), lax.axis_index("section"), lax.axis_index("mp")
    zl, y = dp // NY, lax.rem(dp, NY)
    x, core = section // 2, lax.rem(section, 2)
    z = zh * 2 + zl
    other = 1 - zl

    partner = {"dp": other * NY + y}
    sibling = {"section": x * 2 + 1 - core}

    def at_y(step):
        return {"dp": zl * NY + mod(y + step, NY)}

    def at_x(step):
        return {"section": mod(x + step, NX) * 2 + core}

    def at_z(step):
        there = mod(z + step, NZ)
        return {"dp": lax.rem(there, 2) * NY + y, "mp": there // 2}

    def remote(src, dst, send, recv, device):
        return pltpu.make_async_remote_copy(
            src_ref=src, dst_ref=dst, send_sem=send, recv_sem=recv, device_id=device, device_id_type=MESH
        )

    sent = []

    def push(src, dst, send, recv, device):
        copy = remote(src, dst, send, recv, device)
        copy.start()
        sent.append(copy)

    def arrived(ref, recv):
        remote(ref, ref, recv, recv, sibling).wait_recv()

    barrier = pltpu.get_barrier_semaphore()
    friends = [at_z(d) for d in (1, -1, 2, -2)] + [at_y(d) for d in (1, -1, 2, -2)] + [at_x(1), at_x(-1), sibling]
    for friend in friends:
        pl.semaphore_signal(barrier, inc=1, device_id=friend, device_id_type=MESH)

    def own_columns(h):
        return pl.ds(pl.multiple_of(zl * HEADS * HDIM + h * HDIM, HDIM), HDIM)

    def other_columns(h):
        return pl.ds(pl.multiple_of(other * HEADS * HDIM + h * HDIM, HDIM), HDIM)

    local = []
    for h in range(HEADS):
        for i, w_ref in enumerate((wk_ref, wv_ref)):
            copy = pltpu.make_async_copy(
                w_ref.at[0, :, own_columns(h)], wraw.at[h, zl, y, :, pl.ds(i * HDIM, HDIM)], wl_sem.at[h, i]
            )
            copy.start()
            local.append(copy)
    local_q = []
    for h in range(HEADS):
        for i, w_ref in enumerate((q_ref, g_ref)):
            copy = pltpu.make_async_copy(w_ref.at[0, :, own_columns(h)], qg.at[0, h, i], ql_sem.at[h, i])
            copy.start()
            local_q.append(copy)
    pieces = [enc_ref[s].astype(F32) for s in range(SLOTS)]
    ebuf[zl, zh, x, core] = jnp.concatenate(pieces, axis=0).astype(BF16)
    token = lax.broadcasted_iota(jnp.int32, (8, TOKENS), 1)
    slot_of = (token - CHUNK * ((token * 2731) >> 16)) >> 2
    row = lax.broadcasted_iota(jnp.int32, (8, TOKENS), 0)
    compact = jnp.zeros((8, TOKENS), F32)
    for c in range(BLOCKS):
        first = jnp.where(slot_of == table_ref[pl.ds(0, 1), pl.ds(c, 1)], 1.0, 0.0)
        second = jnp.where(slot_of == table_ref[pl.ds(1, 1), pl.ds(c, 1)], 1.0, 0.0)
        both = first + second * jnp.where(counts_ref[c] > 1, 1.0, 0.0)
        compact = jnp.where(row == c, both, compact)
    mult[0] = compact

    pl.semaphore_wait(barrier, len(friends))

    def chunk(dz, dx, core_of):
        zz = mod(z + dz, NZ)
        return ebuf.at[lax.rem(zz, 2), zz // 2, mod(x + dx, NX), core_of]

    mine = chunk(0, 0, core)
    for d in (1, 7, 2, 6):
        push(mine, mine, z_send.at[d], z_recv.at[d], at_z(d if d < 4 else d - NZ))

    def send_weights():
        for h in range(HEADS):
            for i, w_ref in enumerate((wk_ref, wv_ref)):
                push(
                    w_ref.at[0, :, other_columns(h)], wraw.at[h, zl, y, :, pl.ds(i * HDIM, HDIM)],
                    wz_send.at[h, i], wz_recv.at[h, i], partner,
                )

    def send_rows():
        push(mult.at[0], mult.at[1], mult_sem.at[0], mult_sem.at[1], partner)
        for h in range(HEADS):
            for i, w_ref in enumerate((q_ref, g_ref)):
                push(w_ref.at[0, :, other_columns(h)], qg.at[1, h, i], qz_send.at[h, i], qz_recv.at[h, i], partner)

    def w_own(h):
        for i in range(2):
            local[h * 2 + i].wait()
            arrived(wraw.at[h, other, y, :, pl.ds(i * HDIM, HDIM)], wz_recv.at[h, i])

    def w_step(h, t):
        way = 1 if h % 2 == 0 else -1
        if t == 0:
            w_own(h)
        else:
            arrived(wraw.at[h, :, mod(y - way * t, NY)], wy_recv.at[h, t - 1])
        if t < 4:
            there = wraw.at[h, :, mod(y - way * t, NY)]
            push(there, there, wy_send.at[h, t], wy_recv.at[h, t], at_y(way))
        if 0 < t < 4:
            arrived(wraw.at[h, :, mod(y + way * t, NY)], wy_recv.at[h, 3 + t])
        if t < 3:
            there = wraw.at[h, :, mod(y + way * t, NY)]
            push(there, there, wy_send.at[h, 4 + t], wy_recv.at[h, 4 + t], at_y(-way))

    def to_sibling(ref, d, dx):
        i = d * NX + dx
        push(ref, ref, sib_send.at[i], sib_recv.at[i], sibling)

    def e_first(d):
        ref = chunk(-d, 0, core)
        if d:
            arrived(ref, z_recv.at[d])
        if d == 2:
            push(ref, ref, z_send.at[4], z_recv.at[4], at_z(2))
            push(ref, ref, z_send.at[3], z_recv.at[3], at_z(1))
        if d == 6:
            push(ref, ref, z_send.at[5], z_recv.at[5], at_z(-1))
        push(ref, ref, xp_send.at[d], xp_recv.at[d], at_x(1))
        push(ref, ref, xm_send.at[d], xm_recv.at[d], at_x(-1))
        to_sibling(ref, d, 0)

    def e_second(d):
        ref = chunk(-d, -1, core)
        arrived(ref, xp_recv.at[d])
        if d % 2 == 0:
            push(ref, ref, xo_send.at[d], xo_recv.at[d], at_x(1))
        to_sibling(ref, d, 3)
        ref = chunk(-d, 1, core)
        arrived(ref, xm_recv.at[d])
        if d % 2 == 1:
            push(ref, ref, xo_send.at[d], xo_recv.at[d], at_x(-1))
        to_sibling(ref, d, 1)

    def e_third(d):
        ref = chunk(-d, 2, core)
        arrived(ref, xo_recv.at[d])
        to_sibling(ref, d, 2)

    def w_slot(t):
        for h in range(3):
            w_step(h, t)
        if t >= 3:
            w_step(3, t - 3)

    def each(f, *offsets):
        for d in offsets:
            f(d)

    e_first(0)
    send_weights()
    each(e_first, 1, 7)
    w_slot(0)
    e_second(0)
    each(e_first, 2, 6)
    send_rows()
    each(e_second, 1, 7)
    e_third(0)
    w_slot(1)
    each(e_second, 2, 6)
    each(e_first, 3, 5, 4)
    each(e_third, 1, 7)
    each(e_second, 3, 5)
    each(e_third, 2, 6)
    w_slot(2)
    e_second(4)
    each(e_third, 3, 5, 4)
    w_slot(3)
    for d in range(NZ):
        for dx in range(NX):
            arrived(chunk(-d, dx, 1 - core), sib_recv.at[d * NX + dx])
    for copy in local_q:
        copy.wait()
    for h in range(HEADS):
        for i in range(2):
            arrived(qg.at[1, h, i], qz_recv.at[h, i])
    arrived(mult.at[1], mult_sem.at[1])

    for near in range(2):
        for c in range(BLOCKS):
            times[near, c] = jnp.broadcast_to(mult[near, pl.ds(c, 1), :], (8, TOKENS))

    for r in range(2):

        @pl.loop(0, NZH)
        def _(zz):
            part = ebuf[r, zz].reshape(NX * 2, CHUNK, ENC).astype(F32).reshape(NX * 2 * CHUNK, ENC)
            span = pl.ds(pl.multiple_of(zz * NX * 2 * CHUNK, NX * 2 * CHUNK), NX * 2 * CHUNK)
            tok[r, span, :] = part.astype(BF16)

    scale = HDIM**-0.5

    def project(h):
        @pl.loop(0, 2)
        def _(r):
            kv = jnp.dot(tok[r], wraw[h].reshape(2 * NY * WROWS, 2 * HDIM), preferred_element_type=F32).astype(BF16)
            keys[r] = kv[:, :HDIM]
            values[r] = kv[:, HDIM:]

    def nt(a, b):
        return lax.dot_general(a, b, (((1,), (1,)), ((), ())), preferred_element_type=F32)

    def tn(a, b):
        return lax.dot_general(a, b, (((0,), (0,)), ((), ())), preferred_element_type=F32)

    def attend(h, near):
        r = zl if near == 0 else other
        k, v = keys[r], values[r]
        q, g = qg[near, h, 0], qg[near, h, 1]
        shape = (BLOCKS, BLOCK // 8, 8, TOKENS)
        m = times[near].reshape(BLOCKS, 1, 8, TOKENS)
        scores = nt(q, k).reshape(shape) + jnp.where(m > 0.0, 0.0, -1e30)
        top = jnp.max(scores, axis=3, keepdims=True)
        weights = jnp.exp2((scores - top) * (scale * LOG2E)) * m
        probs = weights * (1.0 / jnp.sum(weights, axis=3, keepdims=True))
        dprob = nt(g, v).reshape(shape)
        delta = jnp.sum(probs * dprob, axis=3, keepdims=True)
        s = (probs * ((dprob - delta) * scale)).reshape(ROWS, TOKENS).astype(BF16)
        p = probs.reshape(ROWS, TOKENS).astype(BF16)
        stage[near, h, 0] = jnp.dot(p, v, preferred_element_type=F32).astype(BF16)
        stage[near, h, 1] = jnp.dot(s, k, preferred_element_type=F32).astype(BF16)
        slots_t[near, pl.ds(0, HDIM), :] = tn(q, s).astype(BF16)
        slots_t[near, pl.ds(HDIM, HDIM), :] = tn(g, p).astype(BF16)

    def send_out(h):
        for i, out in enumerate((ctx_out, gq_out)):
            there = out.at[0, :, own_columns(h)]
            push(stage.at[1, h, i], there, oz_send.at[h, i], oz_recv.at[h, i], partner)
            copy = pltpu.make_async_copy(stage.at[0, h, i], there, ol_sem.at[h, i])
            copy.start()
            ends.append(copy)

    ends = []

    def term(h):
        both = jnp.dot(slots_t[0], tok[zl], preferred_element_type=F32)
        both += jnp.dot(slots_t[1], tok[other], preferred_element_type=F32)
        terms[h] = both.T.reshape(2, NY, WROWS, 2 * HDIM).astype(BF16)

    def rs_step(h, t):
        way = 1 if h % 2 == 0 else -1
        if t < 4:
            there = mod(y + way * (4 - t), NY)
            if t > 0:
                arrived(landed.at[h, t - 1], rs_recv.at[h, t - 1])
                terms[h, :, there] = (terms[h, :, there].astype(F32) + landed[h, t - 1].astype(F32)).astype(BF16)
            push(terms.at[h, :, there], landed.at[h, t], rs_send.at[h, t], rs_recv.at[h, t], at_y(way))
        if t < 3:
            there = mod(y - way * (3 - t), NY)
            if t > 0:
                arrived(landed.at[h, 3 + t], rs_recv.at[h, 3 + t])
                terms[h, :, there] = (terms[h, :, there].astype(F32) + landed[h, 3 + t].astype(F32)).astype(BF16)
            push(terms.at[h, :, there], landed.at[h, 4 + t], rs_send.at[h, 4 + t], rs_recv.at[h, 4 + t], at_y(-way))
        if t == 4:
            rs_end(h, (3, 6))

    def rs_end(h, last):
        whole = terms[h, :, y].astype(F32)
        for i in last:
            arrived(landed.at[h, i], rs_recv.at[h, i])
            whole += landed[h, i].astype(F32)
        total[h] = whole
        for i, out in enumerate((kg_out, vg_out)):
            there = out.at[0, :, own_columns(h)]
            half = pl.ds(i * HDIM, HDIM)
            push(total.at[h, other, :, half], there, fz_send.at[h, i], fz_recv.at[h, i], partner)
            copy = pltpu.make_async_copy(total.at[h, zl, :, half], there, fl_sem.at[h, i])
            copy.start()
            ends.append(copy)

    def rs_fast(h, stage_no):
        def on(step, i, ahead):
            there = terms.at[h, :, mod(y + ahead, NY)]
            push(there, landed.at[h, i], rs_send.at[h, i], rs_recv.at[h, i], at_y(step))

        if stage_no == 0:
            on(2, 0, 4)
            on(1, 1, 3)
            on(-1, 2, -3)
            on(1, 3, 1)
            on(-1, 4, -1)
        elif stage_no == 1:
            for ahead, got, i in ((-2, (2,), 6), (2, (1, 0), 5)):
                there = mod(y + ahead, NY)
                whole = terms[h, :, there].astype(F32)
                for j in got:
                    arrived(landed.at[h, j], rs_recv.at[h, j])
                    whole += landed[h, j].astype(F32)
                terms[h, :, there] = whole.astype(BF16)
                on(ahead, i, ahead)
        else:
            rs_end(h, (3, 4, 6, 5))

    def steps(*which):
        for f, h, t in which:
            f(h, t)

    w, g, f = w_step, rs_step, rs_fast
    after = [
        [(g, 0, 0), (w, 3, 2)],
        [(g, 1, 0), (g, 0, 1), (w, 3, 3)],
        [(f, 2, 0), (g, 1, 1), (g, 0, 2), (w, 3, 4)],
        [(f, 3, 0), (f, 2, 1), (g, 1, 2), (g, 0, 3), (f, 3, 1), (g, 1, 3), (g, 0, 4), (f, 2, 2), (g, 1, 4), (f, 3, 2)],
    ]
    w_slot(4)
    for h in range(HEADS):
        project(h)
        attend(h, 1)
        attend(h, 0)
        send_out(h)
        term(h)
        steps(*after[h])

    for h in range(HEADS):
        for i, (out, grad) in enumerate(((ctx_out, kg_out), (gq_out, vg_out))):
            arrived(out.at[0, :, other_columns(h)], oz_recv.at[h, i])
            arrived(grad.at[0, :, other_columns(h)], fz_recv.at[h, i])
    for copy in ends:
        copy.wait()
    for copy in sent:
        copy.wait_send()


def settle(*refs):
    ins, outs, bufs, sems = refs[:4], refs[4:8], refs[8:12], refs[12]
    inward = [pltpu.make_async_copy(a, b, sems.at[0, i]) for i, (a, b) in enumerate(zip(ins, bufs, strict=True))]
    outward = [pltpu.make_async_copy(a, b, sems.at[1, i]) for i, (a, b) in enumerate(zip(bufs, outs, strict=True))]
    for copy in inward:
        copy.start()
    for copy, later in zip(inward, outward, strict=True):
        copy.wait()
        later.start()
    for copy in outward:
        copy.wait()


def body(queries, grad_context, encodings, table, counts, key_weight, value_weight):
    any_ref = pl.BlockSpec(memory_space=pl.ANY)
    vmem = pl.BlockSpec(memory_space=pltpu.VMEM)
    smem = pl.BlockSpec(memory_space=pltpu.SMEM)
    dma = pltpu.SemaphoreType.DMA
    ring = dma((HEADS, 7))
    pair = dma((HEADS, 2))
    eight = dma((NZ,))
    local = key_weight.shape[2]
    scratch = [
        pltpu.VMEM((2, NZH, NX, 2, CHUNK, ENC), BF16),
        pltpu.VMEM((2, TOKENS, ENC), BF16),
        pltpu.VMEM((HEADS, 2, NY, WROWS, 2 * HDIM), BF16),
        pltpu.VMEM((2, HEADS, 2, ROWS, HDIM), BF16),
        pltpu.VMEM((2, 8, TOKENS), F32),
        pltpu.VMEM((2, BLOCKS, 8, TOKENS), F32),
        pltpu.VMEM((2, TOKENS, HDIM), BF16),
        pltpu.VMEM((2, TOKENS, HDIM), BF16),
        pltpu.VMEM((2, 2 * HDIM, TOKENS), BF16),
        pltpu.VMEM((HEADS, 2, NY, WROWS, 2 * HDIM), BF16),
        pltpu.VMEM((HEADS, 7, 2, WROWS, 2 * HDIM), BF16),
        pltpu.VMEM((2, HEADS, 2, ROWS, HDIM), BF16),
        pltpu.VMEM((HEADS, 2, WROWS, 2 * HDIM), F32),
        dma((2,)), eight, eight, eight, eight, eight, eight, eight, eight, dma((NZ * NX,)), dma((NZ * NX,)),
        pair, pair, pair, ring, ring, pair, pair, pair, ring, ring,
        pair, pair, pair, pair, pair, pair,
    ]
    outs = pl.pallas_call(
        kernel,
        out_shape=(
            jax.ShapeDtypeStruct((1, ROWS, local), BF16),
            jax.ShapeDtypeStruct((1, ROWS, local), BF16),
            jax.ShapeDtypeStruct((1, WROWS, local), F32),
            jax.ShapeDtypeStruct((1, WROWS, local), F32),
        ),
        in_specs=[vmem, smem, any_ref, any_ref, vmem, any_ref, any_ref],
        out_specs=(any_ref,) * 4,
        scratch_shapes=scratch,
        compiler_params=pltpu.CompilerParams(
            collective_id=0, has_side_effects=True, vmem_limit_bytes=56 * 1024 * 1024
        ),
    )(table.T, counts, queries, grad_context, encodings, key_weight, value_weight)
    return pl.pallas_call(
        settle,
        out_shape=tuple(jax.ShapeDtypeStruct(o.shape, o.dtype) for o in outs),
        in_specs=[any_ref] * 4,
        out_specs=(any_ref,) * 4,
        scratch_shapes=[*(pltpu.VMEM(o.shape, o.dtype) for o in outs), dma((2, 4))],
        compiler_params=pltpu.CompilerParams(vmem_limit_bytes=60 * 1024 * 1024),
    )(*outs)


def solution(mesh):
    in_specs = (
        P("section", "dp", "mp"),
        P("section", "dp", "mp"),
        P("dp", ("section", "mp"), None),
        P("dp", None),
        P("dp"),
        P("section", "dp", "mp"),
        P("section", "dp", "mp"),
    )
    out_specs = (
        P("section", "dp", "mp"),
        P("section", "dp", "mp"),
        P("section", "dp", "mp"),
        P("section", "dp", "mp"),
    )
    return jax.shard_map(body, mesh=mesh, in_specs=in_specs, out_specs=out_specs, check_vma=False)
```

time: 131 us -> 80.5 us (0.61)
  Pallas kernels: 123 us -> 79.6 us
  local copies, waits for them, and re-layouts: 7.24 us -> 0 us
    pallas_call x1, Pallas kernels: 123 us -> 77.5 us  [body(): pl.pallas_call(kernel, out_shape=(jax.ShapeDtypeStruct((1, ROWS, local),...]
    unnamed x11 -> x0, local copies, waits for them, and re-layouts: 5.95 us -> none
    pallas_call x0 -> x1, Pallas kernels: none -> 2.09 us  [body(): pl.pallas_call(settle, out_shape=tuple((jax.ShapeDtypeStruct(o.shape, o.d...]
where the time goes in v2:
time: 80.5 us; the launch traced here: 80.2 us
  Pallas kernels  79.6 us (99%)
    pallas_call x1, Pallas kernels, body(): pl.pallas_call(kernel, out_shape=(jax.ShapeDtypeStruct((1, ROWS, local),...  77.5 us
    pallas_call x1, Pallas kernels, body(): pl.pallas_call(settle, out_shape=tuple((jax.ShapeDtypeStruct(o.shape, o.d...  2.09 us

profile of v2, /device:TPU:6, one launch (start us, length us, event | category | flops | bytes accessed | tf_op | source)
XLA Modules:
  0.0 80.2 jit_solution(660751487542032120)
XLA Ops:
  0.6 77.5 %shard_map.102 = (bf16[1,192,1024]{2,1,0:T(8,128)(2,1)}, bf16[1,192,1024]{2,1,0:T(8,128)(2,1)}, f32[1,56,1024]{2,1,0:T(8,128)}, f32[1,56,1024]{2,1,0:T(8,128)}) custom-call(s32[2,3]{1,0:T(2,128)} %bitcast.1, s32[3]{0:T(128)} %counts_ref.1, bf16[1,192,1024]{2,1,0:T(8,128)(2,1)} %q_ref.1, bf16[1,192,1024]{2,1,0:T(8,128)(2,1)} %g_ref.1, ...), custom_call_target="tpu_custom_call" | custom-call | tf_op jit(solution)/shard_map/pallas_call | solution.py:409
  78.1 2.1 %shard_map.103 = (bf16[1,192,1024]{2,1,0:T(8,128)(2,1)}, bf16[1,192,1024]{2,1,0:T(8,128)(2,1)}, f32[1,56,1024]{2,1,0:T(8,128)}, f32[1,56,1024]{2,1,0:T(8,128)}) custom-call(bf16[1,192,1024]{2,1,0:T(8,128)(2,1)} %get-tuple-element.8.refs_0_, bf16[1,192,1024]{2,1,0:T(8,128)(2,1)} %get-tuple-element.9.refs_1_, f32[1,56,1024]{2,1,0:T(8,128)} %get-tuple-element.10.refs_2_, ...), custom_call_target="tpu_custom_call" | custom-call | tf_op jit(solution)/shard_map/pallas_call | solution.py:424

commit v3 on v2

v3 whole, which is shorter than its diff:
```python
import functools

import jax
import jax.numpy as jnp
from jax import lax
from jax.experimental import pallas as pl
from jax.experimental.pallas import tpu as pltpu
from jax.sharding import PartitionSpec as P

MESH = pl.DeviceIdType.MESH
F32, BF16 = jnp.float32, jnp.bfloat16
HDIM = 128
LOG2E = 1.4426950408889634
NY, NX, NZH, NZ = 8, 4, 4, 8
HEADS = 4
SLOTS, PIECE, ENC = 6, 4, 896
CHUNK = SLOTS * PIECE
TOKENS = 768
ROWS, BLOCK, BLOCKS = 192, 64, 3
WROWS = 56
QL, QS, QR, MS, MR, WZ, WY, SS, SR, XS, OL, OS, OR, FL = range(14)
LATE = (3, 4, 5)


def mod(value, n):
    return lax.rem(value + n, n)


def kernel(
    table_ref, counts_ref, q_ref, g_ref, enc_ref, wk_ref, wv_ref,
    ctx_out, gq_out, kg_out, vg_out,
    ebuf, tok, wraw, qg, mult, times, keys, values, slots_t, terms, landed, stage, total,
    one_sem, z_send, z_recv, xp_recv, xm_recv, xo_recv, wl_sem, wz_recv, wy_recv, rs_send, rs_recv,
):
    dp, section, zh = lax.axis_index("dp"), lax.axis_index("section"), lax.axis_index("mp")
    zl, y = dp // NY, lax.rem(dp, NY)
    x, core = section // 2, lax.rem(section, 2)
    z = zh * 2 + zl
    other = 1 - zl

    partner = {"dp": other * NY + y}
    sibling = {"section": x * 2 + 1 - core}

    def at_y(step):
        return {"dp": zl * NY + mod(y + step, NY)}

    def across(step):
        return {"dp": other * NY + mod(y + step, NY)}

    def at_x(step):
        return {"section": mod(x + step, NX) * 2 + core}

    def at_z(step):
        there = mod(z + step, NZ)
        return {"dp": lax.rem(there, 2) * NY + y, "mp": there // 2}

    def remote(src, dst, send, recv, device):
        return pltpu.make_async_remote_copy(
            src_ref=src, dst_ref=dst, send_sem=send, recv_sem=recv, device_id=device, device_id_type=MESH
        )

    def push(src, dst, send, recv, device):
        remote(src, dst, send, recv, device).start()

    def arrived(ref, recv):
        remote(ref, ref, recv, recv, sibling).wait_recv()

    def left(ref, send):
        remote(ref, ref, send, send, sibling).wait_send()

    def moved(ref, sem):
        pltpu.make_async_copy(ref, ref, sem).wait()

    barrier = pltpu.get_barrier_semaphore()
    friends = [at_z(d) for d in (1, -1, 2, -2)] + [at_x(d) for d in (1, -1, 2)] + [sibling]
    friends += [at_y(d) for d in (1, -1, 2, -2)] + [across(d) for d in (1, -1, 2, -2)]
    for friend in friends:
        pl.semaphore_signal(barrier, inc=1, device_id=friend, device_id_type=MESH)

    def own_columns(h):
        return pl.ds(pl.multiple_of(zl * HEADS * HDIM + h * HDIM, HDIM), HDIM)

    def other_columns(h):
        return pl.ds(pl.multiple_of(other * HEADS * HDIM + h * HDIM, HDIM), HDIM)

    for h in range(HEADS):
        for i, w_ref in enumerate((wk_ref, wv_ref)):
            there = wraw.at[h, zl, y, :, pl.ds(i * HDIM, HDIM)]
            pltpu.make_async_copy(w_ref.at[0, :, own_columns(h)], there, wl_sem.at[h // 2]).start()
    for h in range(HEADS):
        for i, w_ref in enumerate((q_ref, g_ref)):
            pltpu.make_async_copy(w_ref.at[0, :, own_columns(h)], qg.at[0, h, i], one_sem.at[QL]).start()
    pieces = [enc_ref[s].astype(F32) for s in range(SLOTS)]
    ebuf[zl, zh, x, core] = jnp.concatenate(pieces, axis=0).astype(BF16)
    token = lax.broadcasted_iota(jnp.int32, (8, TOKENS), 1)
    slot_of = (token - CHUNK * ((token * 2731) >> 16)) >> 2
    row = lax.broadcasted_iota(jnp.int32, (8, TOKENS), 0)
    compact = jnp.zeros((8, TOKENS), F32)
    for c in range(BLOCKS):
        first = jnp.where(slot_of == table_ref[pl.ds(0, 1), pl.ds(c, 1)], 1.0, 0.0)
        second = jnp.where(slot_of == table_ref[pl.ds(1, 1), pl.ds(c, 1)], 1.0, 0.0)
        both = first + second * jnp.where(counts_ref[c] > 1, 1.0, 0.0)
        compact = jnp.where(row == c, both, compact)
    mult[0] = compact

    pl.semaphore_wait(barrier, len(friends))

    def chunk(dz, dx, core_of):
        zz = mod(z + dz, NZ)
        return ebuf.at[lax.rem(zz, 2), zz // 2, mod(x + dx, NX), core_of]

    mine = chunk(0, 0, core)
    for d in (1, 7, 2, 6):
        push(mine, mine, z_send.at[d], z_recv.at[d], at_z(d if d < 4 else d - NZ))

    def send_weights():
        for h in range(HEADS):
            for i, w_ref in enumerate((wk_ref, wv_ref)):
                push(
                    w_ref.at[0, :, other_columns(h)], wraw.at[h, zl, y, :, pl.ds(i * HDIM, HDIM)],
                    one_sem.at[WZ], wz_recv.at[h // 2], partner,
                )

    def send_rows():
        push(mult.at[0], mult.at[1], one_sem.at[MS], one_sem.at[MR], partner)
        for h in range(HEADS):
            for i, w_ref in enumerate((q_ref, g_ref)):
                push(w_ref.at[0, :, other_columns(h)], qg.at[1, h, i], one_sem.at[QS], one_sem.at[QR], partner)

    def w_step(pair, half, t):
        way = -1 if half else 1
        whose = other if half else zl

        def block(back):
            return wraw.at[pl.ds(2 * pair, 2), whose, mod(y - back, NY)]

        def on(back, step, i):
            push(block(back), block(back), one_sem.at[WY], wy_recv.at[pair, half, i], at_y(step))

        if t == 0:
            if half:
                arrived(block(0), wz_recv.at[pair])
            else:
                moved(block(0), wl_sem.at[pair])
        else:
            arrived(block(way * t), wy_recv.at[pair, half, t - 1])
        if t < 4:
            on(way * t, way, t)
        if 0 < t < 4:
            arrived(block(-way * t), wy_recv.at[pair, half, 3 + t])
        if t < 3:
            on(-way * t, -way, 4 + t)

    def to_sibling(ref):
        push(ref, ref, one_sem.at[SS], one_sem.at[SR], sibling)

    def e_first(d):
        ref = chunk(-d, 0, core)
        if d:
            arrived(ref, z_recv.at[d])
        if d == 2:
            push(ref, ref, z_send.at[4], z_recv.at[4], at_z(2))
            push(ref, ref, z_send.at[3], z_recv.at[3], at_z(1))
        if d == 6:
            push(ref, ref, z_send.at[5], z_recv.at[5], at_z(-1))
        push(ref, ref, one_sem.at[XS], xp_recv.at[d], at_x(1))
        push(ref, ref, one_sem.at[XS], xm_recv.at[d], at_x(-1))
        if d in LATE:
            push(ref, ref, one_sem.at[XS], xo_recv.at[d], at_x(2))
        to_sibling(ref)

    def e_second(d):
        ref = chunk(-d, -1, core)
        arrived(ref, xp_recv.at[d])
        if d % 2 == 0 and d not in LATE:
            push(ref, ref, one_sem.at[XS], xo_recv.at[d], at_x(1))
        to_sibling(ref)
        ref = chunk(-d, 1, core)
        arrived(ref, xm_recv.at[d])
        if d % 2 == 1 and d not in LATE:
            push(ref, ref, one_sem.at[XS], xo_recv.at[d], at_x(-1))
        to_sibling(ref)

    def e_third(d):
        ref = chunk(-d, 2, core)
        arrived(ref, xo_recv.at[d])
        to_sibling(ref)

    def each(f, *offsets):
        for d in offsets:
            f(d)

    send_weights()
    w_step(0, 0, 0)
    e_first(0)
    each(e_first, 1, 7)
    w_step(0, 0, 1)
    w_step(0, 1, 0)
    e_second(0)
    each(e_first, 2, 6)
    w_step(1, 0, 0)
    w_step(0, 0, 2)
    w_step(0, 1, 1)
    each(e_second, 1, 7)
    e_third(0)
    each(e_first, 3, 5)
    w_step(1, 1, 0)
    e_first(4)
    send_rows()
    w_step(0, 0, 3)
    w_step(0, 1, 2)
    each(e_second, 2, 6)
    w_step(1, 0, 1)
    each(e_third, 1, 7)
    each(e_second, 3, 5)
    w_step(1, 1, 1)
    w_step(0, 1, 3)
    e_second(4)
    each(e_third, 2, 6)
    w_step(1, 0, 2)
    each(e_third, 3, 5, 4)
    w_step(1, 1, 2)
    w_step(0, 0, 4)
    w_step(0, 1, 4)
    arrived(ebuf.at[0], one_sem.at[SR])
    moved(qg.at[0], one_sem.at[QL])
    arrived(qg.at[1], one_sem.at[QR])
    arrived(mult.at[1], one_sem.at[MR])

    for near in range(2):
        for c in range(BLOCKS):
            times[near, c] = jnp.broadcast_to(mult[near, pl.ds(c, 1), :], (8, TOKENS))

    for r in range(2):

        @pl.loop(0, NZH)
        def _(zz):
            part = ebuf[r, zz].reshape(NX * 2, CHUNK, ENC).astype(F32).reshape(NX * 2 * CHUNK, ENC)
            span = pl.ds(pl.multiple_of(zz * NX * 2 * CHUNK, NX * 2 * CHUNK), NX * 2 * CHUNK)
            tok[r, span, :] = part.astype(BF16)

    scale = HDIM**-0.5

    def project(h):
        @pl.loop(0, 2)
        def _(r):
            kv = jnp.dot(tok[r], wraw[h].reshape(2 * NY * WROWS, 2 * HDIM), preferred_element_type=F32).astype(BF16)
            keys[r] = kv[:, :HDIM]
            values[r] = kv[:, HDIM:]

    def nt(a, b):
        return lax.dot_general(a, b, (((1,), (1,)), ((), ())), preferred_element_type=F32)

    def tn(a, b):
        return lax.dot_general(a, b, (((0,), (0,)), ((), ())), preferred_element_type=F32)

    def attend(h, near):
        r = zl if near == 0 else other
        k, v = keys[r], values[r]
        q, g = qg[near, h, 0], qg[near, h, 1]
        shape = (BLOCKS, BLOCK // 8, 8, TOKENS)
        m = times[near].reshape(BLOCKS, 1, 8, TOKENS)
        scores = nt(q, k).reshape(shape) + jnp.where(m > 0.0, 0.0, -1e30)
        top = jnp.max(scores, axis=3, keepdims=True)
        weights = jnp.exp2((scores - top) * (scale * LOG2E)) * m
        probs = weights * (1.0 / jnp.sum(weights, axis=3, keepdims=True))
        dprob = nt(g, v).reshape(shape)
        delta = jnp.sum(probs * dprob, axis=3, keepdims=True)
        s = (probs * ((dprob - delta) * scale)).reshape(ROWS, TOKENS).astype(BF16)
        p = probs.reshape(ROWS, TOKENS).astype(BF16)
        stage[near, h, 0] = jnp.dot(p, v, preferred_element_type=F32).astype(BF16)
        stage[near, h, 1] = jnp.dot(s, k, preferred_element_type=F32).astype(BF16)
        slots_t[near, pl.ds(0, HDIM), :] = tn(q, s).astype(BF16)
        slots_t[near, pl.ds(HDIM, HDIM), :] = tn(g, p).astype(BF16)

    def send_out(h):
        for i, out in enumerate((ctx_out, gq_out)):
            there = out.at[0, :, own_columns(h)]
            push(stage.at[1, h, i], there, one_sem.at[OS], one_sem.at[OR], partner)
            pltpu.make_async_copy(stage.at[0, h, i], there, one_sem.at[OL]).start()

    def term(h):
        both = jnp.dot(slots_t[0], tok[zl], preferred_element_type=F32)
        both += jnp.dot(slots_t[1], tok[other], preferred_element_type=F32)
        terms[h] = both.T.reshape(2, NY, WROWS, 2 * HDIM).astype(BF16)

    def reduce(h, stage_no):
        for half in range(2):
            way = -1 if half else 1
            whose = other if half else zl

            def on(step, i, ahead, half=half, way=way, whose=whose):
                there = terms.at[h, whose, mod(y + way * ahead, NY)]
                device = across(way * step) if half and i > 2 else at_y(way * step)
                push(there, landed.at[h, half, i], rs_send.at[half], rs_recv.at[h, half, i], device)

            if stage_no == 0:
                on(2, 0, 4)
                on(1, 1, 3)
                on(-1, 2, -3)
                on(1, 3, 1)
                on(-1, 4, -1)
                if half:
                    on(0, 7, 0)
            elif stage_no == 1:
                for ahead, got, i in ((-2, (2,), 6), (2, (1, 0), 5)):
                    there = mod(y + way * ahead, NY)
                    whole = terms[h, whose, there].astype(F32)
                    for j in got:
                        arrived(landed.at[h, half, j], rs_recv.at[h, half, j])
                        whole += landed[h, half, j].astype(F32)
                    terms[h, whose, there] = whole.astype(BF16)
                    on(ahead, i, ahead)
            else:
                last = (3, 4, 6, 5)
                if half:
                    arrived(landed.at[h, 1, 7], rs_recv.at[h, 1, 7])
                    whole = landed[h, 1, 7].astype(F32)
                else:
                    whole = terms[h, zl, y].astype(F32)
                for i in last:
                    arrived(landed.at[h, half, i], rs_recv.at[h, half, i])
                    whole += landed[h, half, i].astype(F32)
                total[h, half] = whole
                columns = other_columns(h) if half else own_columns(h)
                for i, out in enumerate((kg_out, vg_out)):
                    part = total.at[h, half, :, pl.ds(i * HDIM, HDIM)]
                    pltpu.make_async_copy(part, out.at[0, :, columns], one_sem.at[FL]).start()

    for h in range(HEADS):
        if h == 2:
            w_step(1, 0, 4)
            w_step(1, 1, 4)
        project(h)
        if h == 0:
            w_step(1, 0, 3)
            w_step(1, 1, 3)
        if h > 1:
            reduce(h - 2, 1)
        attend(h, 1)
        attend(h, 0)
        send_out(h)
        if h > 2:
            reduce(h - 3, 2)
        term(h)
        reduce(h, 0)
    reduce(HEADS - 2, 1)
    reduce(HEADS - 3, 2)
    reduce(HEADS - 1, 1)
    reduce(HEADS - 2, 2)
    reduce(HEADS - 1, 2)

    arrived(stage.at[1], one_sem.at[OR])
    moved(stage.at[0], one_sem.at[OL])
    moved(total, one_sem.at[FL])
    left(stage.at[1], one_sem.at[OS])
    left(mult.at[0], one_sem.at[MS])
    left(qg.at[1], one_sem.at[QS])
    left(wraw.at[:, 0, 0], one_sem.at[WZ])
    left(wraw.at[:, :, pl.ds(0, 7)], one_sem.at[WY])
    left(ebuf.at[0], one_sem.at[SS])
    left(ebuf.at[0, pl.ds(0, 3)], one_sem.at[XS])
    left(landed.at[:, 0, pl.ds(0, 7)], rs_send.at[0])
    left(landed.at[:, 1], rs_send.at[1])
    for d in range(1, NZ):
        left(chunk(0, 0, core), z_send.at[d])


def settle(*refs):
    ins, outs, bufs, sems = refs[:4], refs[4:8], refs[8:12], refs[12]
    inward = [pltpu.make_async_copy(a, b, sems.at[0, i]) for i, (a, b) in enumerate(zip(ins, bufs, strict=True))]
    outward = [pltpu.make_async_copy(a, b, sems.at[1, i]) for i, (a, b) in enumerate(zip(bufs, outs, strict=True))]
    for copy in inward:
        copy.start()
    for copy, later in zip(inward, outward, strict=True):
        copy.wait()
        later.start()
    for copy in outward:
        copy.wait()


def body(queries, grad_context, encodings, table, counts, key_weight, value_weight):
    any_ref = pl.BlockSpec(memory_space=pl.ANY)
    vmem = pl.BlockSpec(memory_space=pltpu.VMEM)
    smem = pl.BlockSpec(memory_space=pltpu.SMEM)
    dma = pltpu.SemaphoreType.DMA
    eight = dma((NZ,))
    local = key_weight.shape[2]
    scratch = [
        pltpu.VMEM((2, NZH, NX, 2, CHUNK, ENC), BF16),
        pltpu.VMEM((2, TOKENS, ENC), BF16),
        pltpu.VMEM((HEADS, 2, NY, WROWS, 2 * HDIM), BF16),
        pltpu.VMEM((2, HEADS, 2, ROWS, HDIM), BF16),
        pltpu.VMEM((2, 8, TOKENS), F32),
        pltpu.VMEM((2, BLOCKS, 8, TOKENS), F32),
        pltpu.VMEM((2, TOKENS, HDIM), BF16),
        pltpu.VMEM((2, TOKENS, HDIM), BF16),
        pltpu.VMEM((2, 2 * HDIM, TOKENS), BF16),
        pltpu.VMEM((HEADS, 2, NY, WROWS, 2 * HDIM), BF16),
        pltpu.VMEM((HEADS, 2, 8, WROWS, 2 * HDIM), BF16),
        pltpu.VMEM((2, HEADS, 2, ROWS, HDIM), BF16),
        pltpu.VMEM((HEADS, 2, WROWS, 2 * HDIM), F32),
        dma((14,)), eight, eight, eight, eight, eight, dma((2,)), dma((2,)), dma((2, 2, 7)), dma((2,)), dma((HEADS, 2, 8)),
    ]
    outs = pl.pallas_call(
        kernel,
        out_shape=(
            jax.ShapeDtypeStruct((1, ROWS, local), BF16),
            jax.ShapeDtypeStruct((1, ROWS, local), BF16),
            jax.ShapeDtypeStruct((1, WROWS, local), F32),
            jax.ShapeDtypeStruct((1, WROWS, local), F32),
        ),
        in_specs=[vmem, smem, any_ref, any_ref, vmem, any_ref, any_ref],
        out_specs=(any_ref,) * 4,
        scratch_shapes=scratch,
        compiler_params=pltpu.CompilerParams(
            collective_id=0, has_side_effects=True, vmem_limit_bytes=56 * 1024 * 1024
        ),
    )(table.T, counts, queries, grad_context, encodings, key_weight, value_weight)
    return pl.pallas_call(
        settle,
        out_shape=tuple(jax.ShapeDtypeStruct(o.shape, o.dtype) for o in outs),
        in_specs=[any_ref] * 4,
        out_specs=(any_ref,) * 4,
        scratch_shapes=[*(pltpu.VMEM(o.shape, o.dtype) for o in outs), dma((2, 4))],
        compiler_params=pltpu.CompilerParams(vmem_limit_bytes=60 * 1024 * 1024),
    )(*outs)


def solution(mesh):
    in_specs = (
        P("section", "dp", "mp"),
        P("section", "dp", "mp"),
        P("dp", ("section", "mp"), None),
        P("dp", None),
        P("dp"),
        P("section", "dp", "mp"),
        P("section", "dp", "mp"),
    )
    out_specs = (
        P("section", "dp", "mp"),
        P("section", "dp", "mp"),
        P("section", "dp", "mp"),
        P("section", "dp", "mp"),
    )
    return jax.shard_map(body, mesh=mesh, in_specs=in_specs, out_specs=out_specs, check_vma=False)
```

time: 80.5 us -> 72.5 us (0.901)
  the two profiles are of different devices: /device:TPU:6 before, /device:TPU:8 now
where the time goes in v3:
time: 72.5 us; the launch traced here: 72.2 us
  Pallas kernels  71.6 us (99%)
    pallas_call x1, Pallas kernels, body(): pl.pallas_call(kernel, out_shape=(jax.ShapeDtypeStruct((1, ROWS, local),...  69.5 us
    pallas_call x1, Pallas kernels, body(): pl.pallas_call(settle, out_shape=tuple((jax.ShapeDtypeStruct(o.shape, o.d...  2.09 us

profile of v3, /device:TPU:8, one launch (start us, length us, event | category | flops | bytes accessed | tf_op | source)
XLA Modules:
  0.0 72.2 jit_solution(5747256070743726719)
XLA Ops:
  0.6 69.5 %shard_map.102 = (bf16[1,192,1024]{2,1,0:T(8,128)(2,1)}, bf16[1,192,1024]{2,1,0:T(8,128)(2,1)}, f32[1,56,1024]{2,1,0:T(8,128)}, f32[1,56,1024]{2,1,0:T(8,128)}) custom-call(s32[2,3]{1,0:T(2,128)} %bitcast.1, s32[3]{0:T(128)} %counts_ref.1, bf16[1,192,1024]{2,1,0:T(8,128)(2,1)} %q_ref.1, bf16[1,192,1024]{2,1,0:T(8,128)(2,1)} %g_ref.1, ...), custom_call_target="tpu_custom_call" | custom-call | tf_op jit(solution)/shard_map/pallas_call | solution.py:405
  70.2 2.1 %shard_map.103 = (bf16[1,192,1024]{2,1,0:T(8,128)(2,1)}, bf16[1,192,1024]{2,1,0:T(8,128)(2,1)}, f32[1,56,1024]{2,1,0:T(8,128)}, f32[1,56,1024]{2,1,0:T(8,128)}) custom-call(bf16[1,192,1024]{2,1,0:T(8,128)(2,1)} %get-tuple-element.8.refs_0_, bf16[1,192,1024]{2,1,0:T(8,128)(2,1)} %get-tuple-element.9.refs_1_, f32[1,56,1024]{2,1,0:T(8,128)} %get-tuple-element.10.refs_2_, ...), custom_call_target="tpu_custom_call" | custom-call | tf_op jit(solution)/shard_map/pallas_call | solution.py:420

commit v4 on v3

--- a/solution.py
+++ b/solution.py
@@ -18,7 +18,17 @@
 TOKENS = 768
 ROWS, BLOCK, BLOCKS = 192, 64, 3
 WROWS = 56
-QL, QS, QR, MS, MR, WZ, WY, SS, SR, XS, OL, OS, OR, FL = range(14)
+GROUPS = ((0,), (1,), (2, 3))
+GROUP_OF = (0, 1, 2, 2)
+W_TWO = (((0, 2), (0, -2), (0, 1), (0, -1)), ((2, 4), (2, 3), (-2, -3)))
+W_THREE = (((0, 1), (0, -1)), ((1, 3), (1, 2), (-1, -2)), ((3, 4), (-2, -3)))
+W_PLANS = (W_TWO, W_TWO, W_THREE)
+RING = (((4, 3), (-3, -2)), ((3, 2), (-2, -1)), ((2, 1), (-1, 0)), ((1, 0),))
+THREE = (((4, 3), (2, 1), (-3, -2)), ((3, 1), (-2, -1)), ((1, 0), (-1, 0)))
+TWO = (((4, 2), (3, 2), (-3, -2), (1, 0), (-1, 0)), ((2, 0), (-2, 0)))
+PLANS = (RING, RING, THREE, TWO)
+QL, QS, MS, MR, WZ, WY, SS, SR, XS, OL, OS, OR, FL, BX, BZ, BF = range(16)
+FIRST = 640
 LATE = (3, 4, 5)
 
 
@@ -30,7 +40,7 @@
     table_ref, counts_ref, q_ref, g_ref, enc_ref, wk_ref, wv_ref,
     ctx_out, gq_out, kg_out, vg_out,
     ebuf, tok, wraw, qg, mult, times, keys, values, slots_t, terms, landed, stage, total,
-    one_sem, z_send, z_recv, xp_recv, xm_recv, xo_recv, wl_sem, wz_recv, wy_recv, rs_send, rs_recv,
+    one_sem, z_send, z_recv, xp_recv, xm_recv, xo_recv, bx_recv, bz_recv, qr_sem, wl_sem, wz_recv, wy_recv, rs_send, rs_recv,
 ):
     dp, section, zh = lax.axis_index("dp"), lax.axis_index("section"), lax.axis_index("mp")
     zl, y = dp // NY, lax.rem(dp, NY)
@@ -86,7 +96,7 @@
     for h in range(HEADS):
         for i, w_ref in enumerate((wk_ref, wv_ref)):
             there = wraw.at[h, zl, y, :, pl.ds(i * HDIM, HDIM)]
-            pltpu.make_async_copy(w_ref.at[0, :, own_columns(h)], there, wl_sem.at[h // 2]).start()
+            pltpu.make_async_copy(w_ref.at[0, :, own_columns(h)], there, wl_sem.at[GROUP_OF[h]]).start()
     for h in range(HEADS):
         for i, w_ref in enumerate((q_ref, g_ref)):
             pltpu.make_async_copy(w_ref.at[0, :, own_columns(h)], qg.at[0, h, i], one_sem.at[QL]).start()
@@ -107,49 +117,90 @@
 
     def chunk(dz, dx, core_of):
         zz = mod(z + dz, NZ)
-        return ebuf.at[lax.rem(zz, 2), zz // 2, mod(x + dx, NX), core_of]
+        return ebuf.at[lax.rem(zz, 2), zz // 2, mod(x + dx, NX), core_of, :, pl.ds(0, FIRST)]
+
+    rest = pl.ds(FIRST, ENC - FIRST)
+
+    def tail_of(dx):
+        return ebuf.at[zl, zh, mod(x + dx, NX), core, :, rest]
+
+    def tails(dz):
+        zz = mod(z + dz, NZ)
+        return ebuf.at[lax.rem(zz, 2), zz // 2, :, core, :, rest]
 
     mine = chunk(0, 0, core)
-    for d in (1, 7, 2, 6):
-        push(mine, mine, z_send.at[d], z_recv.at[d], at_z(d if d < 4 else d - NZ))
-
-    def send_weights():
-        for h in range(HEADS):
+
+    def send_chunk():
+        for d in (1, 7, 2, 6):
+            push(mine, mine, z_send.at[d], z_recv.at[d], at_z(d if d < 4 else d - NZ))
+
+    def send_tail():
+        for dx in (1, -1, 2):
+            push(tail_of(0), tail_of(0), one_sem.at[BX], bx_recv.at[dx % NX], at_x(dx))
+
+    def tail_first():
+        for dx in (1, 2, 3):
+            arrived(tail_of(-dx), bx_recv.at[dx])
+        for d in (2, 6, 1, 7):
+            push(tails(0), tails(0), one_sem.at[BZ], bz_recv.at[d], at_z(d if d < 4 else d - NZ))
+        to_sibling(tails(0))
+
+    def tail_second():
+        arrived(tails(-2), bz_recv.at[2])
+        push(tails(-2), tails(-2), one_sem.at[BF], bz_recv.at[4], at_z(2))
+        push(tails(-2), tails(-2), one_sem.at[BF], bz_recv.at[3], at_z(1))
+        arrived(tails(2), bz_recv.at[6])
+        push(tails(2), tails(2), one_sem.at[BF], bz_recv.at[5], at_z(-1))
+        for d in (2, 6):
+            to_sibling(tails(-d))
+
+    def tail_third(*which):
+        for d in which:
+            arrived(tails(-d), bz_recv.at[d])
+            to_sibling(tails(-d))
+
+    def send_weights(group):
+        for h in GROUPS[group]:
             for i, w_ref in enumerate((wk_ref, wv_ref)):
                 push(
                     w_ref.at[0, :, other_columns(h)], wraw.at[h, zl, y, :, pl.ds(i * HDIM, HDIM)],
-                    one_sem.at[WZ], wz_recv.at[h // 2], partner,
+                    one_sem.at[WZ], wz_recv.at[group], partner,
                 )
 
-    def send_rows():
-        push(mult.at[0], mult.at[1], one_sem.at[MS], one_sem.at[MR], partner)
-        for h in range(HEADS):
-            for i, w_ref in enumerate((q_ref, g_ref)):
-                push(w_ref.at[0, :, other_columns(h)], qg.at[1, h, i], one_sem.at[QS], one_sem.at[QR], partner)
-
-    def w_step(pair, half, t):
+    def send_rows(h):
+        for i, w_ref in enumerate((q_ref, g_ref)):
+            push(w_ref.at[0, :, other_columns(h)], qg.at[1, h, i], one_sem.at[QS], qr_sem.at[h], partner)
+
+    here = set()
+
+    def w_step(group, half, t):
+        heads, plan = GROUPS[group], W_PLANS[group]
+        edges = [edge for round_ in plan for edge in round_]
         way = -1 if half else 1
         whose = other if half else zl
 
-        def block(back):
-            return wraw.at[pl.ds(2 * pair, 2), whose, mod(y - back, NY)]
-
-        def on(back, step, i):
-            push(block(back), block(back), one_sem.at[WY], wy_recv.at[pair, half, i], at_y(step))
-
-        if t == 0:
-            if half:
-                arrived(block(0), wz_recv.at[pair])
-            else:
-                moved(block(0), wl_sem.at[pair])
+        def block(a):
+            return wraw.at[pl.ds(heads[0], len(heads)), whose, mod(y - way * a, NY)]
+
+        def need(a):
+            if (group, half, a) not in here:
+                here.add((group, half, a))
+                if a:
+                    i = [edge[1] for edge in edges].index(a)
+                    arrived(block(a), wy_recv.at[group, half, i])
+                elif half:
+                    arrived(block(0), wz_recv.at[group])
+                else:
+                    moved(block(0), wl_sem.at[group])
+
+        if t < len(plan):
+            for a, b in plan[t]:
+                need(a)
+                there = wy_recv.at[group, half, edges.index((a, b))]
+                push(block(a), block(a), one_sem.at[WY], there, at_y(way * (b - a)))
         else:
-            arrived(block(way * t), wy_recv.at[pair, half, t - 1])
-        if t < 4:
-            on(way * t, way, t)
-        if 0 < t < 4:
-            arrived(block(-way * t), wy_recv.at[pair, half, 3 + t])
-        if t < 3:
-            on(-way * t, -way, 4 + t)
+            for _, b in edges:
+                need(b)
 
     def to_sibling(ref):
         push(ref, ref, one_sem.at[SS], one_sem.at[SR], sibling)
@@ -190,41 +241,44 @@
         for d in offsets:
             f(d)
 
-    send_weights()
-    w_step(0, 0, 0)
+    def weights(*which):
+        for group, half, t in which:
+            w_step(group, half, t)
+
+    send_weights(0)
+    send_tail()
+    send_chunk()
+    send_weights(1)
+    weights((0, 0, 0), (1, 0, 0), (2, 0, 0))
     e_first(0)
+    tail_first()
     each(e_first, 1, 7)
+    w_step(0, 1, 0)
+    each(e_first, 2, 6)
+    send_weights(2)
     w_step(0, 0, 1)
-    w_step(0, 1, 0)
-    e_second(0)
-    each(e_first, 2, 6)
-    w_step(1, 0, 0)
-    w_step(0, 0, 2)
-    w_step(0, 1, 1)
-    each(e_second, 1, 7)
-    e_third(0)
-    each(e_first, 3, 5)
-    w_step(1, 1, 0)
-    e_first(4)
-    send_rows()
-    w_step(0, 0, 3)
-    w_step(0, 1, 2)
+    each(e_second, 0, 1, 7)
+    weights((1, 1, 0), (1, 0, 1))
+    tail_second()
+    send_rows(0)
+    push(mult.at[0], mult.at[1], one_sem.at[MS], one_sem.at[MR], partner)
+    each(e_third, 0)
+    each(e_first, 3, 5, 4)
     each(e_second, 2, 6)
-    w_step(1, 0, 1)
+    weights((0, 1, 1), (2, 1, 0), (2, 0, 1))
+    tail_third(1, 7)
     each(e_third, 1, 7)
     each(e_second, 3, 5)
-    w_step(1, 1, 1)
-    w_step(0, 1, 3)
+    weights((1, 1, 1), (0, 0, 2))
+    tail_third(3, 5, 4)
+    for h in range(1, HEADS):
+        send_rows(h)
+    each(e_third, 2, 6)
     e_second(4)
-    each(e_third, 2, 6)
-    w_step(1, 0, 2)
     each(e_third, 3, 5, 4)
-    w_step(1, 1, 2)
-    w_step(0, 0, 4)
-    w_step(0, 1, 4)
+    weights((2, 1, 1), (0, 1, 2))
     arrived(ebuf.at[0], one_sem.at[SR])
     moved(qg.at[0], one_sem.at[QL])
-    arrived(qg.at[1], one_sem.at[QR])
     arrived(mult.at[1], one_sem.at[MR])
 
     for near in range(2):
@@ -254,7 +308,7 @@
     def tn(a, b):
         return lax.dot_general(a, b, (((0,), (0,)), ((), ())), preferred_element_type=F32)
 
-    def attend(h, near):
+    def attend_one(h, near):
         r = zl if near == 0 else other
         k, v = keys[r], values[r]
         q, g = qg[near, h, 0], qg[near, h, 1]
@@ -273,7 +327,10 @@
         slots_t[near, pl.ds(0, HDIM), :] = tn(q, s).astype(BF16)
         slots_t[near, pl.ds(HDIM, HDIM), :] = tn(g, p).astype(BF16)
 
-    def send_out(h):
+    def attend(h):
+        arrived(qg.at[1, h], qr_sem.at[h])
+        attend_one(h, 1)
+        attend_one(h, 0)
         for i, out in enumerate((ctx_out, gq_out)):
             there = out.at[0, :, own_columns(h)]
             push(stage.at[1, h, i], there, one_sem.at[OS], one_sem.at[OR], partner)
@@ -285,70 +342,70 @@
         terms[h] = both.T.reshape(2, NY, WROWS, 2 * HDIM).astype(BF16)
 
     def reduce(h, stage_no):
+        plan = PLANS[h]
+        edges = [edge for round_ in plan for edge in round_]
         for half in range(2):
             way = -1 if half else 1
             whose = other if half else zl
 
-            def on(step, i, ahead, half=half, way=way, whose=whose):
-                there = terms.at[h, whose, mod(y + way * ahead, NY)]
-                device = across(way * step) if half and i > 2 else at_y(way * step)
-                push(there, landed.at[h, half, i], rs_send.at[half], rs_recv.at[h, half, i], device)
-
-            if stage_no == 0:
-                on(2, 0, 4)
-                on(1, 1, 3)
-                on(-1, 2, -3)
-                on(1, 3, 1)
-                on(-1, 4, -1)
-                if half:
-                    on(0, 7, 0)
-            elif stage_no == 1:
-                for ahead, got, i in ((-2, (2,), 6), (2, (1, 0), 5)):
-                    there = mod(y + way * ahead, NY)
-                    whole = terms[h, whose, there].astype(F32)
-                    for j in got:
-                        arrived(landed.at[h, half, j], rs_recv.at[h, half, j])
-                        whole += landed[h, half, j].astype(F32)
-                    terms[h, whose, there] = whole.astype(BF16)
-                    on(ahead, i, ahead)
+            def gather(whole, b, h=h, half=half, edges=edges):
+                for i, edge in enumerate(edges):
+                    if edge[1] == b:
+                        arrived(landed.at[h, half, i], rs_recv.at[h, half, i])
+                        whole += landed[h, half, i].astype(F32)
+                return whole
+
+            if stage_no < len(plan):
+                for a, b in plan[stage_no]:
+                    i = edges.index((a, b))
+                    there = mod(y + way * a, NY)
+                    if any(edge[1] == a for edge in edges):
+                        terms[h, whose, there] = gather(terms[h, whose, there].astype(F32), a).astype(BF16)
+                    device = across(way * a) if half and b == 0 else at_y(way * (a - b))
+                    push(terms.at[h, whose, there], landed.at[h, half, i], rs_send.at[half], rs_recv.at[h, half, i], device)
+                if half and stage_no == 0:
+                    push(terms.at[h, other, y], landed.at[h, 1, 7], rs_send.at[1], rs_recv.at[h, 1, 7], partner)
             else:
-                last = (3, 4, 6, 5)
                 if half:
                     arrived(landed.at[h, 1, 7], rs_recv.at[h, 1, 7])
                     whole = landed[h, 1, 7].astype(F32)
                 else:
                     whole = terms[h, zl, y].astype(F32)
-                for i in last:
-                    arrived(landed.at[h, half, i], rs_recv.at[h, half, i])
-                    whole += landed[h, half, i].astype(F32)
-                total[h, half] = whole
+                total[h, half] = gather(whole, 0)
                 columns = other_columns(h) if half else own_columns(h)
                 for i, out in enumerate((kg_out, vg_out)):
                     part = total.at[h, half, :, pl.ds(i * HDIM, HDIM)]
                     pltpu.make_async_copy(part, out.at[0, :, columns], one_sem.at[FL]).start()
 
-    for h in range(HEADS):
-        if h == 2:
-            w_step(1, 0, 4)
-            w_step(1, 1, 4)
-        project(h)
-        if h == 0:
-            w_step(1, 0, 3)
-            w_step(1, 1, 3)
-        if h > 1:
-            reduce(h - 2, 1)
-        attend(h, 1)
-        attend(h, 0)
-        send_out(h)
-        if h > 2:
-            reduce(h - 3, 2)
-        term(h)
-        reduce(h, 0)
-    reduce(HEADS - 2, 1)
-    reduce(HEADS - 3, 2)
-    reduce(HEADS - 1, 1)
-    reduce(HEADS - 2, 2)
-    reduce(HEADS - 1, 2)
+    def sums(*which):
+        for h, stage_no in which:
+            reduce(h, stage_no)
+
+    project(0)
+    w_step(2, 0, 2)
+    attend(0)
+    w_step(2, 1, 2)
+    term(0)
+    reduce(0, 0)
+    weights((1, 0, 2), (1, 1, 2))
+    project(1)
+    attend(1)
+    reduce(0, 1)
+    term(1)
+    reduce(1, 0)
+    weights((2, 0, 3), (2, 1, 3))
+    project(2)
+    reduce(0, 2)
+    attend(2)
+    reduce(1, 1)
+    term(2)
+    reduce(2, 0)
+    reduce(0, 3)
+    project(3)
+    reduce(1, 2)
+    attend(3)
+    term(3)
+    sums((3, 0), (2, 1), (1, 3), (0, 4), (3, 1), (2, 2), (1, 4), (3, 2), (2, 3))
 
     arrived(stage.at[1], one_sem.at[OR])
     moved(stage.at[0], one_sem.at[OL])
@@ -359,7 +416,10 @@
     left(wraw.at[:, 0, 0], one_sem.at[WZ])
     left(wraw.at[:, :, pl.ds(0, 7)], one_sem.at[WY])
     left(ebuf.at[0], one_sem.at[SS])
-    left(ebuf.at[0, pl.ds(0, 3)], one_sem.at[XS])
+    left(ebuf.at[0, pl.ds(0, 3), :, :, :, pl.ds(0, FIRST)], one_sem.at[XS])
+    left(ebuf.at[0, 0, pl.ds(0, 3), 0, :, rest], one_sem.at[BX])
+    left(ebuf.at[0, :, :, 0, :, rest], one_sem.at[BZ])
+    left(ebuf.at[0, pl.ds(0, 3), :, 0, :, rest], one_sem.at[BF])
     left(landed.at[:, 0, pl.ds(0, 7)], rs_send.at[0])
     left(landed.at[:, 1], rs_send.at[1])
     for d in range(1, NZ):
@@ -400,7 +460,8 @@
         pltpu.VMEM((HEADS, 2, 8, WROWS, 2 * HDIM), BF16),
         pltpu.VMEM((2, HEADS, 2, ROWS, HDIM), BF16),
         pltpu.VMEM((HEADS, 2, WROWS, 2 * HDIM), F32),
-        dma((14,)), eight, eight, eight, eight, eight, dma((2,)), dma((2,)), dma((2, 2, 7)), dma((2,)), dma((HEADS, 2, 8)),
+        dma((16,)), eight, eight, eight, eight, eight, dma((NX,)), eight, dma((HEADS,)), dma((3,)), dma((3,)), dma((3, 2, 7)), dma((2,)),
+        dma((HEADS, 2, 8)),
     ]
     outs = pl.pallas_call(
         kernel,

time: 72.5 us -> 70.3 us (0.970)
  the two profiles are of different devices: /device:TPU:8 before, /device:TPU:6 now
where the time goes in v4:
time: 70.3 us; the launch traced here: 70 us
  Pallas kernels  69.4 us (99%)
    pallas_call x1, Pallas kernels, body(): pl.pallas_call(kernel, out_shape=(jax.ShapeDtypeStruct((1, ROWS, local),...  67.3 us
    pallas_call x1, Pallas kernels, body(): pl.pallas_call(settle, out_shape=tuple((jax.ShapeDtypeStruct(o.shape, o.d...  2.09 us

profile of v4, /device:TPU:6, one launch (start us, length us, event | category | flops | bytes accessed | tf_op | source)
XLA Modules:
  0.0 70.0 jit_solution(9524882247791053823)
XLA Ops:
  0.6 67.3 %shard_map.102 = (bf16[1,192,1024]{2,1,0:T(8,128)(2,1)}, bf16[1,192,1024]{2,1,0:T(8,128)(2,1)}, f32[1,56,1024]{2,1,0:T(8,128)}, f32[1,56,1024]{2,1,0:T(8,128)}) custom-call(s32[2,3]{1,0:T(2,128)} %bitcast.1, s32[3]{0:T(128)} %counts_ref.1, bf16[1,192,1024]{2,1,0:T(8,128)(2,1)} %q_ref.1, bf16[1,192,1024]{2,1,0:T(8,128)(2,1)} %g_ref.1, ...), custom_call_target="tpu_custom_call" | custom-call | tf_op jit(solution)/shard_map/pallas_call | solution.py:466
  67.9 2.1 %shard_map.103 = (bf16[1,192,1024]{2,1,0:T(8,128)(2,1)}, bf16[1,192,1024]{2,1,0:T(8,128)(2,1)}, f32[1,56,1024]{2,1,0:T(8,128)}, f32[1,56,1024]{2,1,0:T(8,128)}) custom-call(bf16[1,192,1024]{2,1,0:T(8,128)(2,1)} %get-tuple-element.8.refs_0_, bf16[1,192,1024]{2,1,0:T(8,128)(2,1)} %get-tuple-element.9.refs_1_, f32[1,56,1024]{2,1,0:T(8,128)} %get-tuple-element.10.refs_2_, ...), custom_call_target="tpu_custom_call" | custom-call | tf_op jit(solution)/shard_map/pallas_call | solution.py:481

commit v5 on v4

--- a/solution.py
+++ b/solution.py
@@ -24,9 +24,8 @@
 W_THREE = (((0, 1), (0, -1)), ((1, 3), (1, 2), (-1, -2)), ((3, 4), (-2, -3)))
 W_PLANS = (W_TWO, W_TWO, W_THREE)
 RING = (((4, 3), (-3, -2)), ((3, 2), (-2, -1)), ((2, 1), (-1, 0)), ((1, 0),))
-THREE = (((4, 3), (2, 1), (-3, -2)), ((3, 1), (-2, -1)), ((1, 0), (-1, 0)))
 TWO = (((4, 2), (3, 2), (-3, -2), (1, 0), (-1, 0)), ((2, 0), (-2, 0)))
-PLANS = (RING, RING, THREE, TWO)
+PLANS = (RING, RING, TWO, TWO)
 QL, QS, MS, MR, WZ, WY, SS, SR, XS, OL, OS, OR, FL, BX, BZ, BF = range(16)
 FIRST = 640
 LATE = (3, 4, 5)
@@ -405,7 +404,7 @@
     reduce(1, 2)
     attend(3)
     term(3)
-    sums((3, 0), (2, 1), (1, 3), (0, 4), (3, 1), (2, 2), (1, 4), (3, 2), (2, 3))
+    sums((3, 0), (2, 1), (1, 3), (0, 4), (3, 1), (2, 2), (1, 4), (3, 2))
 
     arrived(stage.at[1], one_sem.at[OR])
     moved(stage.at[0], one_sem.at[OL])

time: 70.3 us -> 69.7 us (level)
  Pallas kernels: 69.4 us -> 68.2 us
    pallas_call x1, Pallas kernels: 67.3 us -> 66.1 us  [body(): pl.pallas_call(kernel, out_shape=(jax.ShapeDtypeStruct((1, ROWS, local),...]
where the time goes in v5:
time: 69.7 us; the launch traced here: 68.8 us
  Pallas kernels  68.2 us (98%)
    pallas_call x1, Pallas kernels, body(): pl.pallas_call(kernel, out_shape=(jax.ShapeDtypeStruct((1, ROWS, local),...  66.1 us
    pallas_call x1, Pallas kernels, body(): pl.pallas_call(settle, out_shape=tuple((jax.ShapeDtypeStruct(o.shape, o.d...  2.09 us

profile of v5, /device:TPU:6, one launch (start us, length us, event | category | flops | bytes accessed | tf_op | source)
XLA Modules:
  0.0 68.8 jit_solution(18267472589913282292)
XLA Ops:
  0.6 66.1 %shard_map.102 = (bf16[1,192,1024]{2,1,0:T(8,128)(2,1)}, bf16[1,192,1024]{2,1,0:T(8,128)(2,1)}, f32[1,56,1024]{2,1,0:T(8,128)}, f32[1,56,1024]{2,1,0:T(8,128)}) custom-call(s32[2,3]{1,0:T(2,128)} %bitcast.1, s32[3]{0:T(128)} %counts_ref.1, bf16[1,192,1024]{2,1,0:T(8,128)(2,1)} %q_ref.1, bf16[1,192,1024]{2,1,0:T(8,128)(2,1)} %g_ref.1, ...), custom_call_target="tpu_custom_call" | custom-call | tf_op jit(solution)/shard_map/pallas_call | solution.py:465
  66.7 2.1 %shard_map.103 = (bf16[1,192,1024]{2,1,0:T(8,128)(2,1)}, bf16[1,192,1024]{2,1,0:T(8,128)(2,1)}, f32[1,56,1024]{2,1,0:T(8,128)}, f32[1,56,1024]{2,1,0:T(8,128)}) custom-call(bf16[1,192,1024]{2,1,0:T(8,128)(2,1)} %get-tuple-element.8.refs_0_, bf16[1,192,1024]{2,1,0:T(8,128)(2,1)} %get-tuple-element.9.refs_1_, f32[1,56,1024]{2,1,0:T(8,128)} %get-tuple-element.10.refs_2_, ...), custom_call_target="tpu_custom_call" | custom-call | tf_op jit(solution)/shard_map/pallas_call | solution.py:480

commit v6 on v5

--- a/solution.py
+++ b/solution.py
@@ -267,8 +267,9 @@
     weights((0, 1, 1), (2, 1, 0), (2, 0, 1))
     tail_third(1, 7)
     each(e_third, 1, 7)
+    w_step(1, 1, 1)
     each(e_second, 3, 5)
-    weights((1, 1, 1), (0, 0, 2))
+    w_step(0, 0, 2)
     tail_third(3, 5, 4)
     for h in range(1, HEADS):
         send_rows(h)

time: 69.7 us -> 70.3 us (level)
  no operation moved by 1% of the time
where the time goes in v6:
time: 70.3 us; the launch traced here: 69 us
  Pallas kernels  68.4 us (97%)
    pallas_call x1, Pallas kernels, body(): pl.pallas_call(kernel, out_shape=(jax.ShapeDtypeStruct((1, ROWS, local),...  66.3 us
    pallas_call x1, Pallas kernels, body(): pl.pallas_call(settle, out_shape=tuple((jax.ShapeDtypeStruct(o.shape, o.d...  2.09 us

profile of v6, /device:TPU:6, one launch (start us, length us, event | category | flops | bytes accessed | tf_op | source)
XLA Modules:
  0.0 69.0 jit_solution(1126038711881245204)
XLA Ops:
  0.6 66.3 %shard_map.102 = (bf16[1,192,1024]{2,1,0:T(8,128)(2,1)}, bf16[1,192,1024]{2,1,0:T(8,128)(2,1)}, f32[1,56,1024]{2,1,0:T(8,128)}, f32[1,56,1024]{2,1,0:T(8,128)}) custom-call(s32[2,3]{1,0:T(2,128)} %bitcast.1, s32[3]{0:T(128)} %counts_ref.1, bf16[1,192,1024]{2,1,0:T(8,128)(2,1)} %q_ref.1, bf16[1,192,1024]{2,1,0:T(8,128)(2,1)} %g_ref.1, ...), custom_call_target="tpu_custom_call" | custom-call | tf_op jit(solution)/shard_map/pallas_call | solution.py:466
  66.9 2.1 %shard_map.103 = (bf16[1,192,1024]{2,1,0:T(8,128)(2,1)}, bf16[1,192,1024]{2,1,0:T(8,128)(2,1)}, f32[1,56,1024]{2,1,0:T(8,128)}, f32[1,56,1024]{2,1,0:T(8,128)}) custom-call(bf16[1,192,1024]{2,1,0:T(8,128)(2,1)} %get-tuple-element.8.refs_0_, bf16[1,192,1024]{2,1,0:T(8,128)(2,1)} %get-tuple-element.9.refs_1_, f32[1,56,1024]{2,1,0:T(8,128)} %get-tuple-element.10.refs_2_, ...), custom_call_target="tpu_custom_call" | custom-call | tf_op jit(solution)/shard_map/pallas_call | solution.py:481
